TPU v7x, 128 devices: a whole 4x4x4 slice. The times are simulated.
128 devices in a mesh: row: 16 (over x, z), col: 8 (over y, core).
Axes of the slice: x: 4, y: 4, z: 4, core: 2. Of those that a mesh axis runs over, the one named last changes fastest.
Arguments:
- cam_jac: float32 [8192, 36, 128], P(('row', 'col')), may hold values from -6 to 6
- pt_jac: float32 [8192, 12, 128], P(('row', 'col')), may hold values from -6 to 6
- resid: float32 [8192, 4, 128], P(('row', 'col')), may hold values from -0.3 to 0.3
- damping: float32 [8192, 128], P(('row', 'col')), may hold values from 0.5 to 4
- cams: int32 [8192, 2, 128], P(('row', 'col')), may hold values from 0 to 127
- block_pair: int32 [8192, 1], P(('row', 'col')), may hold values from 0 to 63; in each aligned block of 64 rows (0 to 63, 64 to 127, ...) at most 2 rows name the same one
- pair_sides: int32 [64, 2], replicated, may hold values from 0 to 127, as said below
- cluster_home: int32 [32], replicated, may hold values from 0 to 31, each once
Outputs:
- schur_blocks: float32 [128, 1152, 1152], P(('row', 'col'))
- reduced_rhs: float32 [32, 1152], P('row', 'col')
Inputs may be any that keep to these rules, and one draw needn't show every extreme that they name: `pair_sides`: every side 0 to 127 appears exactly once. `block_pair`: among the 64 blocks of one device no pair is named more than 2 times, a bound that some block reaches.
All inputs are finite; a program needn't handle non-finite values.
Results may differ from a plain program's by a relative error of at most 0.0003.
Values sent between devices are 32-bit elements; how exact they have to be, the bound alone decides.
No kernel may reach another device: no remote copies, remote signals or barrier semaphores. Data moves between devices by JAX's collectives and lax.ppermute only.
A program may use at most 192 MiB of HBM per device.

v0:
```python
import jax
import jax.numpy as jnp
from jax import lax
from jax.sharding import PartitionSpec as P

CAMS = 128
CL_ROW = 2


def invert_three(matrix):
    cofactor_rows = []
    for row_pick in range(3):
        entries = []
        for col_pick in range(3):
            entries.append(
                matrix[:, (col_pick + 1) % 3, (row_pick + 1) % 3]
                * matrix[:, (col_pick + 2) % 3, (row_pick + 2) % 3]
                - matrix[:, (col_pick + 1) % 3, (row_pick + 2) % 3]
                * matrix[:, (col_pick + 2) % 3, (row_pick + 1) % 3]
            )
        cofactor_rows.append(jnp.stack(entries, axis=1))
    adjugate = jnp.stack(cofactor_rows, axis=1)
    determinant = (
        matrix[:, 0, 0] * adjugate[:, 0, 0]
        + matrix[:, 0, 1] * adjugate[:, 1, 0]
        + matrix[:, 0, 2] * adjugate[:, 2, 0]
    )
    return adjugate / determinant[:, None, None, :]


def point_terms(cam_jac, pt_jac, resid, damping):
    blocks_here = cam_jac.shape[0]
    points_here = cam_jac.shape[-1]
    camera_rows = cam_jac.reshape(blocks_here, 2, 2, 9, points_here)
    point_rows = pt_jac.reshape(blocks_here, 2, 2, 3, points_here)
    errors = resid.reshape(blocks_here, 2, 2, points_here)
    hessian = jnp.sum(
        point_rows[:, :, :, :, None, :] * point_rows[:, :, :, None, :, :], axis=(1, 2)
    )
    hessian = hessian + damping[:, None, None, :] * jnp.eye(3, dtype=jnp.float32)[None, :, :, None]
    inverse = invert_three(hessian)
    coupling = jnp.sum(camera_rows[:, :, :, :, None, :] * point_rows[:, :, :, None, :, :], axis=2)
    cam_grad = jnp.sum(camera_rows * errors[:, :, :, None, :], axis=2)
    point_grad = jnp.sum(point_rows * errors[:, :, :, None, :], axis=(1, 2))
    shifted = jnp.sum(inverse * point_grad[:, None, :, :], axis=2)
    scaled = jnp.sum(coupling[:, :, :, :, None, :] * inverse[:, None, None, :, :, :], axis=3)
    reduced = cam_grad - jnp.sum(coupling * shifted[:, None, None, :, :], axis=3)
    return (coupling, scaled, reduced)


def lookup(table, index):
    hits = index[..., None] == jnp.arange(table.shape[0], dtype=jnp.int32)
    return jnp.sum(jnp.where(hits, table, 0), axis=-1)


def local(cam_jac, pt_jac, resid, damping, cams, block_pair, pair_sides, cluster_home):
    blocks_here = cam_jac.shape[0]
    points_here = cam_jac.shape[-1]
    width = 9 * CAMS
    row_count = lax.axis_size("row")
    col_count = lax.axis_size("col")
    devices = row_count * col_count
    neighbours = col_count // CL_ROW
    cluster_count = cluster_home.shape[0]
    most = max(2, 2 * blocks_here // pair_sides.shape[0])
    coupling, scaled, reduced = point_terms(cam_jac, pt_jac, resid, damping)
    pair_ids = block_pair[:, 0]
    sides = jnp.stack(
        [lookup(pair_sides[:, 0], pair_ids), lookup(pair_sides[:, 1], pair_ids)], axis=1
    )
    homes = lookup(cluster_home, sides // neighbours)
    targets = homes * neighbours + sides % neighbours
    rhs_rows_index = (homes[:, :, None] * CAMS + cams).reshape(-1)
    rhs_values = jnp.transpose(reduced, (0, 1, 3, 2)).reshape(-1, 9)
    partial_value = (
        jnp.zeros((cluster_count * CAMS, 9), jnp.float32).at[rhs_rows_index].add(rhs_values)
    )
    partial_value = partial_value.reshape(cluster_count, width)
    total_rhs = lax.psum(partial_value, ("row", "col"))
    share = width // col_count
    reduced_rhs = lax.dynamic_slice(
        total_rhs, (lax.axis_index("row") * CL_ROW, lax.axis_index("col") * share), (CL_ROW, share)
    )
    partner = coupling[:, ::-1]
    cam_pair = jnp.stack([cams, cams[:, ::-1]], axis=2)
    product = jnp.sum(scaled[:, :, :, None, :, :] * partner[:, :, None, :, :, :], axis=4)
    payload = product.reshape(blocks_here, 2, 81, points_here)
    features = payload.shape[2]
    order = jnp.arange(blocks_here, dtype=jnp.int32)
    same_pair = pair_ids[:, None] == pair_ids[None, :]
    earlier = order[:, None] > order[None, :]
    rank = jnp.sum(jnp.where(same_pair & earlier, 1, 0), axis=1).astype(jnp.int32)
    slot_of = targets * most + rank[:, None]
    table = (
        jnp.full((devices * most,), -1, jnp.int32)
        .at[slot_of.reshape(-1)]
        .set(jnp.arange(blocks_here * 2, dtype=jnp.int32))
    )
    filled = table >= 0
    source = jnp.maximum(table, 0)
    outgoing = jnp.where(
        filled[:, None, None], payload.reshape(blocks_here * 2, features, points_here)[source], 0.0
    )
    out_cams = jnp.where(
        filled[:, None, None], cam_pair.reshape(blocks_here * 2, 2, points_here)[source], 0
    ).astype(jnp.float32)
    arrived, arrived_cams = (
        lax.all_to_all(
            outgoing.reshape(devices, most, features, points_here),
            ("row", "col"),
            split_axis=0,
            concat_axis=0,
            tiled=True,
        ),
        lax.all_to_all(
            out_cams.reshape(devices, most, 2, points_here),
            ("row", "col"),
            split_axis=0,
            concat_axis=0,
            tiled=True,
        ),
    )
    arrived = arrived.reshape(row_count, -1, features, points_here)
    arrived_cams = arrived_cams.reshape(row_count, -1, 2, points_here)

    def add_group(group, total):
        values = lax.dynamic_index_in_dim(arrived, group, 0, keepdims=False)
        cam_values = lax.dynamic_index_in_dim(arrived_cams, group, 0, keepdims=False).astype(
            jnp.int32
        )
        count_here = values.shape[0]
        terms = values.reshape(count_here, 9, 9, points_here)
        tile_rows = jnp.transpose(terms, (0, 3, 1, 2)).reshape(-1, 81)
        tile_index = (cam_values[:, 0, :] * CAMS + cam_values[:, 1, :]).reshape(-1)
        return total.at[tile_index].add(tile_rows)

    total = lax.fori_loop(0, row_count, add_group, jnp.zeros((CAMS * CAMS, 81), jnp.float32))
    total = jnp.transpose(total.reshape(CAMS, CAMS, 9, 9), (0, 2, 1, 3)).reshape(width, width)
    schur_blocks = (-total).reshape(1, width, width)
    return (schur_blocks, reduced_rhs)


def solution(mesh):
    return jax.shard_map(
        local,
        mesh=mesh,
        in_specs=(
            P(("row", "col"), None, None),
            P(("row", "col"), None, None),
            P(("row", "col"), None, None),
            P(("row", "col"), None),
            P(("row", "col"), None, None),
            P(("row", "col"), None),
            P(),
            P(),
        ),
        out_specs=(P(("row", "col"), None, None), P("row", "col")),
        check_vma=False,
    )
```

profile of v0, /device:TPU:1, one launch (start us, length us, event | category | flops | bytes accessed | tf_op | source)
XLA Modules:
  0.0 931.1 jit_solution(16961277867132312947)
XLA Ops:
  28.3 5.0 copy.141
  33.3 5.7 copy.142
  39.0 8.3 gather_fusion.1
  47.3 16.9 %copy_select_fusion = f32[128,2,81,128]{3,1,2,0:T(2,128)} fusion(f32[128,2,81,128]{3,2,1,0:T(8,128)} %bitcast.94, pred[128,2]{1,0:T(8,128)(4,1)S(1)} %broadcast_in_dim.97), kind=kLoop, calls=%fused_computation.12 | loop fusion | flops 2654208 | bytes 21233920 | tf_op jit(solution)/shard_map/jit(_where)/select_n | solution.py:101
  64.2 11.9 %all-to-all-start.1 = ((f32[128,2,81,128]{3,1,2,0:T(2,128)}), f32[128,2,81,128]{3,1,2,0:T(2,128)}, u32[]{:S(2)}, u32[]{:S(2)}) async-start(f32[128,2,81,128]{3,1,2,0:T(2,128)} %copy_select_fusion), calls=%async_computation.1 | async-start | bytes 21233664 | tf_op jit(solution)/shard_map/all_to_all | solution.py:108
  84.0 128.6 %all-to-all-done.1 = f32[128,2,81,128]{3,1,2,0:T(2,128)} async-done(((f32[128,2,81,128]{3,1,2,0:T(2,128)}), f32[128,2,81,128]{3,1,2,0:T(2,128)}, u32[]{:S(2)}, u32[]{:S(2)}) %all-to-all-start.1) | async-done | bytes 10616864 | tf_op jit(solution)/shard_map/all_to_all | solution.py:108
  212.6 11.5 %all-to-all-start = ((f32[128,2,2,128]{3,2,1,0:T(2,128)}), f32[128,2,2,128]{3,2,1,0:T(2,128)S(1)}, u32[]{:S(2)}, u32[]{:S(2)}) async-start(f32[128,2,2,128]{3,2,1,0:T(2,128)} %select_convert_fusion), calls=%async_computation | async-start | bytes 524288 | tf_op jit(solution)/shard_map/all_to_all | solution.py:115
  224.2 4.7 copy.153
  228.9 88.3 %scatter_custom_fusion.2 = f32[4096,9]{1,0:T(8,128)S(1)} fusion(s32[16384]{0:T(1024)S(1)} %bitcast.113, f32[16384,9]{1,0:T(8,128)} %bitcast.100, f32[]{:T(128)} %constant.90.clone.1), kind=kCustom, calls=%fused_computation.18 | custom fusion | flops 147456 | bytes 147968 | tf_op jit(solution)/shard_map/scatter-add | solution.py:76
  318.8 141.7 %all-reduce.2.cloned.1.call-done = f32[32,1152]{1,0:T(8,128)} async-done(((f32[32,1152]{1,0:T(8,128)}), f32[32,1152]{1,0:T(8,128)}) %all-reduce.2.cloned.1.call-update) | async-done | bytes 147472 | tf_op jit(solution)/shard_map/psum | solution.py:79
  461.9 9.7 %copy.144 = f32[128,2,81,128]{3,1,0,2:T(2,128)} copy(f32[128,2,81,128]{3,1,2,0:T(2,128)} %all-to-all-done.1) | data formatting | bytes 21233664 | tf_op jit(solution)/shard_map/all_to_all | solution.py:108
  475.2 341.4 %while.13 = (s32[]{:T(128)}, f32[16384,81]{1,0:T(8,128)}, f32[16,16,2,128]{3,2,1,0:T(2,128)S(1)}, f32[16,16,81,128]{3,1,0,2:T(8,128)}, s32[]{:T(128)}, /*index=5*/f32[]{:T(128)}) while((s32[]{:T(128)}, f32[16384,81]{1,0:T(8,128)}, f32[16,16,2,128]{3,2,1,0:T(2,128)S(1)}, f32[16,16,81,128]{3,1,0,2:T(8,128)}, s32[]{:T(128)}, ...), condition=%wide.region_11.12_spmd, body=%wide.region_9.11_spmd.sunk | while | flops 180226 | bytes 7536729 | solution.py:137
  477.0 19.1 %scatter_fusion = f32[16384,81]{1,0:T(8,128)} fusion(f32[16384,81]{1,0:T(8,128)} %get-tuple-element.163, s32[2048]{0:T(1024)S(1)} %bitcast.107, f32[2048,81]{1,0:T(8,128)S(1)} %copy.162), kind=kCustom, calls=%fused_computation.2.clone.1 | custom fusion | flops 165888 | bytes 1998848 | tf_op jit(solution)/shard_map/while/body/eval_jaxpr/scatter-add | solution.py:135
  498.0 19.4 %scatter_fusion = f32[16384,81]{1,0:T(8,128)} fusion(f32[16384,81]{1,0:T(8,128)} %get-tuple-element.163, s32[2048]{0:T(1024)S(1)} %bitcast.107, f32[2048,81]{1,0:T(8,128)S(1)} %copy.162), kind=kCustom, calls=%fused_computation.2.clone.1 | custom fusion | flops 165888 | bytes 1998848 | tf_op jit(solution)/shard_map/while/body/eval_jaxpr/scatter-add | solution.py:135
  519.2 19.4 %scatter_fusion = f32[16384,81]{1,0:T(8,128)} fusion(f32[16384,81]{1,0:T(8,128)} %get-tuple-element.163, s32[2048]{0:T(1024)S(1)} %bitcast.107, f32[2048,81]{1,0:T(8,128)S(1)} %copy.162), kind=kCustom, calls=%fused_computation.2.clone.1 | custom fusion | flops 165888 | bytes 1998848 | tf_op jit(solution)/shard_map/while/body/eval_jaxpr/scatter-add | solution.py:135
  540.4 19.4 %scatter_fusion = f32[16384,81]{1,0:T(8,128)} fusion(f32[16384,81]{1,0:T(8,128)} %get-tuple-element.163, s32[2048]{0:T(1024)S(1)} %bitcast.107, f32[2048,81]{1,0:T(8,128)S(1)} %copy.162), kind=kCustom, calls=%fused_computation.2.clone.1 | custom fusion | flops 165888 | bytes 1998848 | tf_op jit(solution)/shard_map/while/body/eval_jaxpr/scatter-add | solution.py:135
  561.7 19.4 %scatter_fusion = f32[16384,81]{1,0:T(8,128)} fusion(f32[16384,81]{1,0:T(8,128)} %get-tuple-element.163, s32[2048]{0:T(1024)S(1)} %bitcast.107, f32[2048,81]{1,0:T(8,128)S(1)} %copy.162), kind=kCustom, calls=%fused_computation.2.clone.1 | custom fusion | flops 165888 | bytes 1998848 | tf_op jit(solution)/shard_map/while/body/eval_jaxpr/scatter-add | solution.py:135
  582.9 19.7 %scatter_fusion = f32[16384,81]{1,0:T(8,128)} fusion(f32[16384,81]{1,0:T(8,128)} %get-tuple-element.163, s32[2048]{0:T(1024)S(1)} %bitcast.107, f32[2048,81]{1,0:T(8,128)S(1)} %copy.162), kind=kCustom, calls=%fused_computation.2.clone.1 | custom fusion | flops 165888 | bytes 1998848 | tf_op jit(solution)/shard_map/while/body/eval_jaxpr/scatter-add | solution.py:135
  604.4 19.7 %scatter_fusion = f32[16384,81]{1,0:T(8,128)} fusion(f32[16384,81]{1,0:T(8,128)} %get-tuple-element.163, s32[2048]{0:T(1024)S(1)} %bitcast.107, f32[2048,81]{1,0:T(8,128)S(1)} %copy.162), kind=kCustom, calls=%fused_computation.2.clone.1 | custom fusion | flops 165888 | bytes 1998848 | tf_op jit(solution)/shard_map/while/body/eval_jaxpr/scatter-add | solution.py:135
  626.0 19.7 %scatter_fusion = f32[16384,81]{1,0:T(8,128)} fusion(f32[16384,81]{1,0:T(8,128)} %get-tuple-element.163, s32[2048]{0:T(1024)S(1)} %bitcast.107, f32[2048,81]{1,0:T(8,128)S(1)} %copy.162), kind=kCustom, calls=%fused_computation.2.clone.1 | custom fusion | flops 165888 | bytes 1998848 | tf_op jit(solution)/shard_map/while/body/eval_jaxpr/scatter-add | solution.py:135
  647.5 19.7 %scatter_fusion = f32[16384,81]{1,0:T(8,128)} fusion(f32[16384,81]{1,0:T(8,128)} %get-tuple-element.163, s32[2048]{0:T(1024)S(1)} %bitcast.107, f32[2048,81]{1,0:T(8,128)S(1)} %copy.162), kind=kCustom, calls=%fused_computation.2.clone.1 | custom fusion | flops 165888 | bytes 1998848 | tf_op jit(solution)/shard_map/while/body/eval_jaxpr/scatter-add | solution.py:135
  669.0 19.7 %scatter_fusion = f32[16384,81]{1,0:T(8,128)} fusion(f32[16384,81]{1,0:T(8,128)} %get-tuple-element.163, s32[2048]{0:T(1024)S(1)} %bitcast.107, f32[2048,81]{1,0:T(8,128)S(1)} %copy.162), kind=kCustom, calls=%fused_computation.2.clone.1 | custom fusion | flops 165888 | bytes 1998848 | tf_op jit(solution)/shard_map/while/body/eval_jaxpr/scatter-add | solution.py:135
  690.5 19.4 %scatter_fusion = f32[16384,81]{1,0:T(8,128)} fusion(f32[16384,81]{1,0:T(8,128)} %get-tuple-element.163, s32[2048]{0:T(1024)S(1)} %bitcast.107, f32[2048,81]{1,0:T(8,128)S(1)} %copy.162), kind=kCustom, calls=%fused_computation.2.clone.1 | custom fusion | flops 165888 | bytes 1998848 | tf_op jit(solution)/shard_map/while/body/eval_jaxpr/scatter-add | solution.py:135
  711.7 19.4 %scatter_fusion = f32[16384,81]{1,0:T(8,128)} fusion(f32[16384,81]{1,0:T(8,128)} %get-tuple-element.163, s32[2048]{0:T(1024)S(1)} %bitcast.107, f32[2048,81]{1,0:T(8,128)S(1)} %copy.162), kind=kCustom, calls=%fused_computation.2.clone.1 | custom fusion | flops 165888 | bytes 1998848 | tf_op jit(solution)/shard_map/while/body/eval_jaxpr/scatter-add | solution.py:135
  732.9 19.7 %scatter_fusion = f32[16384,81]{1,0:T(8,128)} fusion(f32[16384,81]{1,0:T(8,128)} %get-tuple-element.163, s32[2048]{0:T(1024)S(1)} %bitcast.107, f32[2048,81]{1,0:T(8,128)S(1)} %copy.162), kind=kCustom, calls=%fused_computation.2.clone.1 | custom fusion | flops 165888 | bytes 1998848 | tf_op jit(solution)/shard_map/while/body/eval_jaxpr/scatter-add | solution.py:135
  754.5 19.7 %scatter_fusion = f32[16384,81]{1,0:T(8,128)} fusion(f32[16384,81]{1,0:T(8,128)} %get-tuple-element.163, s32[2048]{0:T(1024)S(1)} %bitcast.107, f32[2048,81]{1,0:T(8,128)S(1)} %copy.162), kind=kCustom, calls=%fused_computation.2.clone.1 | custom fusion | flops 165888 | bytes 1998848 | tf_op jit(solution)/shard_map/while/body/eval_jaxpr/scatter-add | solution.py:135
  776.0 19.4 %scatter_fusion = f32[16384,81]{1,0:T(8,128)} fusion(f32[16384,81]{1,0:T(8,128)} %get-tuple-element.163, s32[2048]{0:T(1024)S(1)} %bitcast.107, f32[2048,81]{1,0:T(8,128)S(1)} %copy.162), kind=kCustom, calls=%fused_computation.2.clone.1 | custom fusion | flops 165888 | bytes 1998848 | tf_op jit(solution)/shard_map/while/body/eval_jaxpr/scatter-add | solution.py:135
  797.2 19.4 %scatter_fusion = f32[16384,81]{1,0:T(8,128)} fusion(f32[16384,81]{1,0:T(8,128)} %get-tuple-element.163, s32[2048]{0:T(1024)S(1)} %bitcast.107, f32[2048,81]{1,0:T(8,128)S(1)} %copy.162), kind=kCustom, calls=%fused_computation.2.clone.1 | custom fusion | flops 165888 | bytes 1998848 | tf_op jit(solution)/shard_map/while/body/eval_jaxpr/scatter-add | solution.py:135
  816.6 5.7 neg.19
  822.3 8.6 copy.146
  837.3 38.1 %copy.147 = f32[128,9,128,9]{3,2,1,0:T(8,128)} copy(f32[128,9,128,9]{2,0,3,1:T(8,128)} %bitcast.98) | data formatting | bytes 10616832 | tf_op jit(solution)/shard_map/neg | solution.py:139
  875.4 48.9 %neg.22 = f32[1,1152,1152]{2,1,0:T(8,128)} reshape(f32[128,9,128,9]{3,2,1,0:T(8,128)} %copy.147) | data formatting | bytes 10616832 | tf_op jit(solution)/shard_map/neg | solution.py:139
  (160 shorter events, 70.6 us)
Async XLA Ops:
  14.1 1.3 copy-start.1
  17.7 1.7 copy-start.2
  33.3 5.7 copy-start.4
  64.2 11.9 %copy-start.5 = (s32[64,2]{0,1:T(2,128)S(1)}, s32[64,2]{0,1:T(2,128)}, u32[]{:S(2)}) copy-start(s32[64,2]{0,1:T(2,128)} %get-tuple-element.123) | copy-start | bytes 1540
  64.2 12.6 %copy-start.3 = (s32[64,2,128]{2,1,0:T(2,128)S(1)}, s32[64,2,128]{2,1,0:T(2,128)}, u32[]{:S(2)}) copy-start(s32[64,2,128]{2,1,0:T(2,128)} %param.14) | copy-start | bytes 196612
  64.2 14.6 %copy-start = (f32[64,36,128]{2,0,1:T(8,128)S(1)}, f32[64,36,128]{2,0,1:T(8,128)}, u32[]{:S(2)}) copy-start(f32[64,36,128]{2,0,1:T(8,128)} %param.10) | copy-start | bytes 3538948
  64.2 148.4 %all-to-all-start.1 = ((f32[128,2,81,128]{3,1,2,0:T(2,128)}), f32[128,2,81,128]{3,1,2,0:T(2,128)}, u32[]{:S(2)}, u32[]{:S(2)}) async-start(f32[128,2,81,128]{3,1,2,0:T(2,128)} %copy_select_fusion), calls=%async_computation.1 | async-start | bytes 21233664 | tf_op jit(solution)/shard_map/all_to_all | solution.py:108
  212.6 259.0 %all-to-all-start = ((f32[128,2,2,128]{3,2,1,0:T(2,128)}), f32[128,2,2,128]{3,2,1,0:T(2,128)S(1)}, u32[]{:S(2)}, u32[]{:S(2)}) async-start(f32[128,2,2,128]{3,2,1,0:T(2,128)} %select_convert_fusion), calls=%async_computation | async-start | bytes 524288 | tf_op jit(solution)/shard_map/all_to_all | solution.py:115
  224.1 236.4 %all-reduce.2.cloned.1.call-start = ((), (), s32[]{:S(2)}) async-start(), calls=%async_computation.2 | async-start | bytes 294912 | tf_op jit(solution)/shard_map/psum | solution.py:79
Sparse Core Ops, SparseCore 0:
  318.9 141.5 all-reduce.1
where the time goes:
time: 935 us; the launch traced here: 931 us
  other arithmetic  446 us (48%)
  waiting for transfers between devices  270 us (29%)
  local copies, waits for them, and re-layouts  176 us (19%)
  starting transfers between devices  23.4 us (3%)
  between operations  14.3 us (2%)
    scatter-add x16, other arithmetic, add_group(): return total.at[tile_index].add(tile_rows)  312 us
    psum x1, waiting for transfers between devices, local(): total_rhs = lax.psum(partial_value, ('row', 'col'))  142 us
    all_to_all x1, waiting for transfers between devices, local(): lax.all_to_all(outgoing.reshape(devices, most, features, points_here), ('...  129 us
    neg x3, local copies, waits for them, and re-layouts, local(): schur_blocks = (-total).reshape(1, width, width)  95.6 us
    scatter-add x1, other arithmetic, local(): jnp.zeros((cluster_count * CAMS, 9), jnp.float32).at[rhs_rows_index]  88.3 us
    while x48, local copies, waits for them, and re-layouts  22.9 us
  transfers between devices with their start and end apart: 3, of which 2 were waited for; matrix products, arithmetic and copies ran while one was open for 12% of the time, Pallas kernels for 0%

commit v1 on v0

v1 whole, which is shorter than its diff:
```python
import functools

import jax
import jax.numpy as jnp
from jax import lax
from jax.experimental import pallas as pl
from jax.experimental.pallas import tpu as pltpu
from jax.sharding import PartitionSpec as P

CAMS = 128
PTS = 128
WIDTH = 9 * CAMS
NBR = 4
SIDES = 128
CLUSTERS = 32
BLK = 40
GROUP = 8
TABLES = 4
UNROLL = 32
FINAL = 8
FEATS = 88
VMEM_LIMIT = 60 * 2**20
RC = ("row", "col")


def inverse_of(pt_ref, damp_ref):
    jp = [[[pt_ref[:, 6 * o + 3 * r + k, :] for k in range(3)] for r in range(2)] for o in range(2)]
    damp = damp_ref[...]

    def entry(a, b):
        total = jp[0][0][a] * jp[0][0][b]
        for o, r in ((0, 1), (1, 0), (1, 1)):
            total = total + jp[o][r][a] * jp[o][r][b]
        return total + damp if a == b else total

    v00, v01, v02, v11, v12, v22 = (entry(a, b) for a, b in ((0, 0), (0, 1), (0, 2), (1, 1), (1, 2), (2, 2)))
    a00 = v11 * v22 - v12 * v12
    a01 = v02 * v12 - v01 * v22
    a02 = v01 * v12 - v02 * v11
    a11 = v00 * v22 - v02 * v02
    a12 = v01 * v02 - v00 * v12
    a22 = v00 * v11 - v01 * v01
    det = v00 * a00 + v01 * a01 + v02 * a02
    inv = [[a00 / det, a01 / det, a02 / det], [a01 / det, a11 / det, a12 / det], [a02 / det, a12 / det, a22 / det]]
    return jp, inv


def slot_of(side, home_ref):
    return home_ref[side // NBR] * NBR + side % NBR


def pack_kernel(bp_ref, ps_ref, home_ref, cam_ref, pt_ref, damp_ref, cams_ref, out0_ref, out1_ref, mix_ref, seen_ref):
    blocks = cam_ref.shape[0]
    out0_ref[...] = jnp.zeros_like(out0_ref)
    out1_ref[...] = jnp.zeros_like(out1_ref)
    jp, inv = inverse_of(pt_ref, damp_ref)
    for r in range(2):
        left = [sum(jp[0][r][k] * inv[k][m] for k in range(3)) for m in range(3)]
        for q in range(2):
            mix_ref[2 * r + q] = -sum(left[m] * jp[1][q][m] for m in range(3))

    def clear(i, carry):
        seen_ref[i] = 0
        return carry

    lax.fori_loop(0, seen_ref.shape[0], clear, 0)

    def one(t, carry):
        pair = bp_ref[t, 0]
        rank = seen_ref[pair]
        seen_ref[pair] = rank + 1
        first, second = slot_of(ps_ref[pair, 0], home_ref), slot_of(ps_ref[pair, 1], home_ref)
        row0, row1 = cam_ref[t, 0:9, :], cam_ref[t, 9:18, :]
        other = [cam_ref[t, 18:27, :], cam_ref[t, 27:36, :]]
        mix = [mix_ref[k, pl.ds(t, 1), :] for k in range(4)]
        mixed = [row0 * mix[q] + row1 * mix[2 + q] for q in range(2)]
        ids = cams_ref[t].astype(jnp.float32)

        def put(out_ref, slot, a, b, ca, cb):
            out_ref[slot, 0:8, :] = a[0][0:8]
            out_ref[slot, 8:16, :] = a[1][0:8]
            out_ref[slot, 16:24, :] = b[0][0:8]
            out_ref[slot, 24:32, :] = b[1][0:8]
            out_ref[slot, 32:33, :] = a[0][8:9]
            out_ref[slot, 33:34, :] = a[1][8:9]
            out_ref[slot, 34:35, :] = b[0][8:9]
            out_ref[slot, 35:36, :] = b[1][8:9]
            out_ref[slot, 36:37, :] = ca
            out_ref[slot, 37:38, :] = cb

        def both(out_ref):
            put(out_ref, first, mixed, other, ids[0:1], ids[1:2])
            put(out_ref, second, other, mixed, ids[1:2], ids[0:1])

        @pl.when(rank == 0)
        def _():
            both(out0_ref)

        @pl.when(rank != 0)
        def _():
            both(out1_ref)

        return carry

    lax.fori_loop(0, blocks, one, 0)


def rhs_kernel(bp_ref, ps_ref, home_ref, cam_ref, pt_ref, res_ref, damp_ref, cams_ref, out_ref, w_ref):
    blocks = cam_ref.shape[0]
    out_ref[...] = jnp.zeros_like(out_ref)
    jp, inv = inverse_of(pt_ref, damp_ref)
    err = [[res_ref[:, 2 * o + r, :] for r in range(2)] for o in range(2)]
    gp = [sum(jp[o][r][k] * err[o][r] for o in range(2) for r in range(2)) for k in range(3)]
    z = [sum(inv[k][m] * gp[m] for m in range(3)) for k in range(3)]
    for o in range(2):
        for r in range(2):
            w_ref[2 * o + r] = err[o][r] - sum(jp[o][r][k] * z[k] for k in range(3))
    number = lax.broadcasted_iota(jnp.int32, (CAMS, PTS), 0)

    def one(t, carry):
        pair = bp_ref[t, 0]
        for o in range(2):
            home = home_ref[ps_ref[pair, o] // NBR]
            b = cam_ref[t, 18 * o : 18 * o + 9, :] * w_ref[2 * o, pl.ds(t, 1), :]
            b = b + cam_ref[t, 18 * o + 9 : 18 * o + 18, :] * w_ref[2 * o + 1, pl.ds(t, 1), :]
            b = jnp.concatenate([b, jnp.zeros((7, PTS), jnp.float32)], axis=0)
            high = b.astype(jnp.bfloat16)
            low = (b - high.astype(jnp.float32)).astype(jnp.bfloat16)
            hit = jnp.where(number == cams_ref[t, o : o + 1, :], 1.0, 0.0).astype(jnp.bfloat16)
            added = lax.dot_general(
                jnp.concatenate([high, low], axis=0), hit, (((1,), (1,)), ((), ())), preferred_element_type=jnp.float32
            )
            out_ref[home] = out_ref[home] + (added[0:16] + added[16:32])
        return carry

    lax.fori_loop(0, blocks, one, 0)


def expand(block):
    a0, a1, b0, b1 = block[0:8], block[8:16], block[16:24], block[24:32]
    a08, a18, b08, b18 = block[32:33], block[33:34], block[34:35], block[35:36]
    rows = [a0 * b0[j : j + 1] + a1 * b1[j : j + 1] for j in range(8)]
    rows.append(a0 * b08 + a1 * b18)
    rows.append(a08 * b0 + a18 * b1)
    rows.append(jnp.broadcast_to(a08 * b08 + a18 * b18, (8, PTS)))
    return rows


def accumulate(idx_ref, in_ref, pay_ref, tabs):
    for g in range(GROUP):
        rows = expand(in_ref[g])
        rows.append(jnp.zeros((CAMS - FEATS, PTS), jnp.float32))
        pay_ref[pl.ds(g * PTS, PTS), :] = jnp.concatenate(rows, axis=0).T

    def body(q, carry):
        base = pl.multiple_of(q * UNROLL, UNROLL)
        for u in range(UNROLL):
            i = idx_ref[0, 0, base + u]
            tab = tabs[u % TABLES]
            tab[pl.ds(i, 1), :] = tab[pl.ds(i, 1), :] + pay_ref[pl.ds(base + u, 1), :]
        return carry

    lax.fori_loop(0, GROUP * PTS // UNROLL, body, 0)


def first_kernel(steps, idx_ref, in_ref, out_ref, pay_ref, *tabs):
    step = pl.program_id(0)
    part = out_ref.shape[0]

    @pl.when(step == 0)
    def _():
        for tab in tabs:
            tab[...] = jnp.zeros_like(tab)

    @pl.when(step < steps)
    def _():
        accumulate(idx_ref, in_ref, pay_ref, tabs)

    @pl.when(step >= steps)
    def _():
        rows = pl.ds(pl.multiple_of((step - steps) * part, part), part)
        total = tabs[0][rows, :]
        for tab in tabs[1:]:
            total = total + tab[rows, :]
        out_ref[...] = total


def last_kernel(steps, idx_ref, in_ref, start_ref, out_ref, pay_ref, spread_ref, wide_ref, *tabs):
    step = pl.program_id(0)

    @pl.when(step == 0)
    def _():
        for tab in tabs:
            tab[...] = jnp.zeros_like(tab)
        source = lax.broadcasted_iota(jnp.int32, (CAMS, WIDTH), 0) * 9
        lane = lax.broadcasted_iota(jnp.int32, (CAMS, WIDTH), 1)
        spread = jnp.where((lane >= source) & (lane < source + 9), 1.0, 0.0).astype(jnp.bfloat16)
        spread_ref[0:CAMS, :] = spread
        spread_ref[CAMS : 2 * CAMS, :] = spread

    @pl.when(step < steps)
    def _():
        accumulate(idx_ref, in_ref, pay_ref, tabs)

    @pl.when(step >= steps)
    def _():
        base = pl.multiple_of((step - steps) * FINAL * CAMS, FINAL * CAMS)
        parts = []
        for c in range(FINAL):
            rows = pl.ds(base + c * CAMS, CAMS)
            total = start_ref[rows, :]
            for tab in tabs:
                total = total + tab[rows, :]
            total = total.T[0:FEATS]
            high = total.astype(jnp.bfloat16)
            low = (total - high.astype(jnp.float32)).astype(jnp.bfloat16)
            parts.append(jnp.concatenate([high, low], axis=1))
        wide_ref[...] = jnp.dot(jnp.concatenate(parts, axis=0), spread_ref[...], preferred_element_type=jnp.float32)
        lane = lax.broadcasted_iota(jnp.int32, (8, WIDTH), 1)
        which = lane % 9
        sub = lax.broadcasted_iota(jnp.int32, (8, WIDTH), 0)
        for c in range(FINAL):
            at = c * FEATS
            eight = wide_ref[at : at + 8, :]
            for j in range(1, 9):
                eight = jnp.where(which == j, wide_ref[at + 8 * j : at + 8 * j + 8, :], eight)
            last = jnp.sum(jnp.where(which == sub, wide_ref[at + 72 : at + 80, :], 0.0), axis=0, keepdims=True)
            last = jnp.where(which[0:1] == 8, wide_ref[at + 80 : at + 81, :], last)
            out_ref[0, 9 * c : 9 * c + 8, :] = eight
            out_ref[0, 9 * c + 8 : 9 * c + 9, :] = last


def params(**more):
    return pltpu.CompilerParams(vmem_limit_bytes=VMEM_LIMIT, **more)


def index_of(arrived):
    cell = arrived[:, 36, :] * CAMS + arrived[:, 37, :]
    return cell.astype(jnp.int32).reshape(SIDES // GROUP, 1, GROUP * PTS)


def local(cam_jac, pt_jac, resid, damping, cams, block_pair, pair_sides, cluster_home):
    smem = pl.BlockSpec(memory_space=pltpu.SMEM)
    vmem = pl.BlockSpec(memory_space=pltpu.VMEM)
    blocks = cam_jac.shape[0]
    sent = jax.ShapeDtypeStruct((SIDES, BLK, PTS), jnp.float32)
    out0, out1 = pl.pallas_call(
        pack_kernel,
        in_specs=[smem] * 3 + [vmem] * 4,
        out_specs=[vmem, vmem],
        out_shape=[sent, sent],
        scratch_shapes=[pltpu.VMEM((4, blocks, PTS), jnp.float32), pltpu.SMEM((pair_sides.shape[0],), jnp.int32)],
        compiler_params=params(),
        name="pack",
    )(block_pair, pair_sides, cluster_home, cam_jac, pt_jac, damping, cams)
    in0 = lax.all_to_all(out0, RC, 0, 0, tiled=True)
    in1 = lax.all_to_all(out1, RC, 0, 0, tiled=True)

    partial = pl.pallas_call(
        rhs_kernel,
        in_specs=[smem] * 3 + [vmem] * 5,
        out_specs=vmem,
        out_shape=jax.ShapeDtypeStruct((CLUSTERS, 16, CAMS), jnp.float32),
        scratch_shapes=[pltpu.VMEM((4, blocks, PTS), jnp.float32)],
        compiler_params=params(),
        cost_estimate=pl.CostEstimate(flops=10**8, bytes_accessed=3 * 10**6, transcendentals=0),
        name="rhs",
    )(block_pair, pair_sides, cluster_home, cam_jac, pt_jac, resid, damping, cams)
    rows, cols = lax.axis_size("row"), lax.axis_size("col")
    shares = partial[:, 0:9].reshape(rows, CLUSTERS // rows, 9, cols, CAMS // cols)
    shares = jnp.transpose(shares, (0, 3, 1, 2, 4)).reshape(rows * cols, -1)
    share = lax.psum_scatter(shares, RC, scatter_dimension=0, tiled=True)
    share = share.reshape(CLUSTERS // rows, 9, CAMS // cols)
    reduced_rhs = jnp.transpose(share, (0, 2, 1)).reshape(CLUSTERS // rows, WIDTH // cols)

    steps = SIDES // GROUP
    cells = CAMS * CAMS
    part = 2048
    spec_idx = pl.BlockSpec((1, 1, GROUP * PTS), lambda s: (jnp.minimum(s, steps - 1), 0, 0), memory_space=pltpu.SMEM)
    spec_in = pl.BlockSpec((GROUP, BLK, PTS), lambda s: (jnp.minimum(s, steps - 1), 0, 0))
    tabs = [pltpu.VMEM((cells, PTS), jnp.float32)] * TABLES
    pay = pltpu.VMEM((GROUP * PTS, PTS), jnp.float32)
    cost = pl.CostEstimate(flops=6 * 10**9, bytes_accessed=12 * 10**6, transcendentals=0)
    total = pl.pallas_call(
        functools.partial(first_kernel, steps),
        grid=(steps + cells // part,),
        in_specs=[spec_idx, spec_in],
        out_specs=pl.BlockSpec((part, PTS), lambda s: (jnp.maximum(s - steps, 0), 0)),
        out_shape=jax.ShapeDtypeStruct((cells, PTS), jnp.float32),
        scratch_shapes=[pay] + tabs,
        compiler_params=params(),
        cost_estimate=cost,
        name="first",
    )(index_of(in0), in0)
    schur = pl.pallas_call(
        functools.partial(last_kernel, steps),
        grid=(steps + CAMS // FINAL,),
        in_specs=[spec_idx, spec_in, vmem],
        out_specs=pl.BlockSpec((1, 9 * FINAL, WIDTH), lambda s: (0, jnp.maximum(s - steps, 0), 0)),
        out_shape=jax.ShapeDtypeStruct((1, WIDTH, WIDTH), jnp.float32),
        scratch_shapes=[
            pay,
            pltpu.VMEM((2 * CAMS, WIDTH), jnp.bfloat16),
            pltpu.VMEM((FINAL * FEATS, WIDTH), jnp.float32),
        ]
        + tabs,
        compiler_params=params(),
        cost_estimate=cost,
        name="last",
    )(index_of(in1), in1, total)
    return schur, reduced_rhs


def solution(mesh):
    return jax.shard_map(
        local,
        mesh=mesh,
        in_specs=(
            P(RC, None, None),
            P(RC, None, None),
            P(RC, None, None),
            P(RC, None),
            P(RC, None, None),
            P(RC, None),
            P(),
            P(),
        ),
        out_specs=(P(RC, None, None), P("row", "col")),
        check_vma=False,
    )
```

time: 935 us -> 344 us (0.37)
  other arithmetic: 446 us -> 4 us
  local copies, waits for them, and re-layouts: 176 us -> 12.8 us
  waiting for transfers between devices: 270 us -> 146 us
  Pallas kernels: 0 us -> 113 us
  blocking collectives: 0 us -> 47.7 us
  starting transfers between devices: 23.4 us -> 5.72 us
    scatter-add x17 -> x0, other arithmetic: 400 us -> none  [the longest x16 312 us: add_group(): return total.at[tile_index].add(tile_rows)]
    unnamed x1 -> x2, waiting for transfers between devices: 0.02 us -> 146 us
    psum x1 -> x0, waiting for transfers between devices: 142 us -> none  [local(): total_rhs = lax.psum(partial_value, ('row', 'col'))]
    all_to_all x2 -> x1, waiting for transfers between devices: 129 us -> 0.01 us  [local(): in1 = lax.all_to_all(out1, RC, 0, 0, tiled=True)]
    pallas_call x0 -> x4, Pallas kernels: none -> 113 us  [the longest x1 54.8 us: local(): pl.pallas_call(functools.partial(last_kernel, steps), grid=(steps + CAMS...]
    neg x3 -> x0, local copies, waits for them, and re-layouts: 95.6 us -> none  [local(): schur_blocks = (-total).reshape(1, width, width)]
    all_to_all x0 -> x1, blocking collectives: none -> 47.7 us  [local(): in0 = lax.all_to_all(out0, RC, 0, 0, tiled=True)]
    while x48 -> x0, local copies, waits for them, and re-layouts: 22.9 us -> none
  transfers between devices with their start and end apart: 3 -> 2, of which waited for: 2 -> 1; matrix products, arithmetic and copies ran while one was open for 12% -> 2% of each run, Pallas kernels for 0% -> 4%
where the time goes in v1:
time: 344 us; the launch traced here: 343 us
  waiting for transfers between devices  146 us (42%)
  Pallas kernels  113 us (33%)
  blocking collectives  47.7 us (14%)
  between operations  14.1 us (4%)
  local copies, waits for them, and re-layouts  12.8 us (4%)
  starting transfers between devices  5.72 us (2%)
  other arithmetic  4 us (1%)
    unnamed x2, waiting for transfers between devices  146 us
    pallas_call x1, Pallas kernels, local(): pl.pallas_call(functools.partial(last_kernel, steps), grid=(steps + CAMS...  54.8 us
    all_to_all x1, blocking collectives, local(): in0 = lax.all_to_all(out0, RC, 0, 0, tiled=True)  47.7 us
    pallas_call x1, Pallas kernels, local(): pl.pallas_call(functools.partial(first_kernel, steps), grid=(steps + cell...  36.1 us
    pallas_call x1, Pallas kernels, local(): pl.pallas_call(rhs_kernel, in_specs=[smem] * 3 + [vmem] * 5, out_specs=vm...  13.8 us
    unnamed x5, local copies, waits for them, and re-layouts  8.54 us
    pallas_call x1, Pallas kernels, local(): pl.pallas_call(pack_kernel, in_specs=[smem] * 3 + [vmem] * 4, out_specs=[...  8.35 us
  transfers between devices with their start and end apart: 2, of which 1 were waited for; matrix products, arithmetic and copies ran while one was open for 2% of the time, Pallas kernels for 4%

profile of v1, /device:TPU:1, one launch (start us, length us, event | category | flops | bytes accessed | tf_op | source)
XLA Modules:
  0.0 343.0 jit_solution(7671744601721130315)
XLA Ops:
  7.2 1.3 copy.33.bp_ref
  8.5 1.4 copy.34.ps_ref
  9.9 2.0 copy.36.pt_ref
  11.9 3.0 copy.35.cam_ref
  15.0 8.4 %pack.1 = (f32[128,40,128]{2,1,0:T(8,128)}, f32[128,40,128]{2,1,0:T(8,128)}) custom-call(s32[64,1]{1,0:T(8,128)} %copy.33.bp_ref, s32[64,2]{1,0:T(8,128)} %copy.34.ps_ref, s32[32]{0:T(128)} %home_ref.3, f32[64,36,128]{2,1,0:T(8,128)} %copy.35.cam_ref, f32[64,12,128]{2,1,0:T(8,128)} %copy.36.pt_ref, f32[64,128]{1,0:T(8,128)} %damp_ref.3, s32[64,2,128]{2,1,0:T(2,128)} %cams_ref.3), custom_call_target="tpu_custom_call" | custom-call | tf_op jit(solution)/shard_map/pack/pallas_call | solution.py:247
  23.3 47.7 %all_to_all.10.in_ref = f32[128,40,128]{2,1,0:T(8,128)} all-to-all(f32[128,40,128]{2,1,0:T(8,128)} %get-tuple-element.5), channel_id=1, replica_groups=mesh['row'=16,'col'=8] {'row','col'}, dimensions={0} | all-to-all | bytes 5242880 | tf_op jit(solution)/shard_map/all_to_all | solution.py:256
  71.0 5.5 %all-to-all-start = ((f32[128,40,128]{2,1,0:T(8,128)}), f32[128,40,128]{2,1,0:T(8,128)}, u32[]{:S(2)}, u32[]{:S(2)}) async-start(f32[128,40,128]{2,1,0:T(8,128)} %get-tuple-element.4), calls=%async_computation | async-start | bytes 5242880 | tf_op jit(solution)/shard_map/all_to_all | solution.py:257
  76.5 0.2 all-reduce.3.cloned.1.call-start
  76.8 13.8 %rhs.2 = f32[32,16,128]{2,1,0:T(8,128)} custom-call(s32[64,1]{1,0:T(8,128)} %copy.33.bp_ref, s32[64,2]{1,0:T(8,128)} %copy.34.ps_ref, s32[32]{0:T(128)} %home_ref.3, f32[64,36,128]{2,1,0:T(8,128)} %copy.35.cam_ref, f32[64,12,128]{2,1,0:T(8,128)} %copy.36.pt_ref, f32[64,4,128]{2,1,0:T(4,128)} %res_ref.1, f32[64,128]{1,0:T(8,128)} %damp_ref.3, ...), custom_call_target="tpu_custom_call" | custom-call | flops 100000000 | bytes 3000000 | tf_op jit(solution)/shard_map/rhs/pallas_call | solution.py:259
  90.5 1.0 copy.43
  91.5 0.3 reshape.72
  91.9 0.7 copy.44
  92.6 1.3 reshape.73
  94.0 0.0 all-reduce.3.cloned.1.call-update
  94.0 145.6 %all-reduce.3.cloned.1.call-done = f32[128,288]{1,0:T(8,128)} async-done(((f32[128,288]{1,0:T(8,128)}), f32[128,288]{1,0:T(8,128)}) %all-reduce.3.cloned.1.call-update) | async-done | bytes 147472
  239.6 0.7 dynamic-slice_reduce_fusion
  240.3 0.1 reshape.74
  240.4 0.1 copy.45
  240.5 0.7 reshape.75
  241.2 2.0 fusion
  243.2 0.0 all-to-all-done.in_ref
  243.2 2.0 fusion.1
  245.2 36.1 %first.1.start_ref = f32[16384,128]{1,0:T(8,128)} custom-call(s32[16,1,1024]{2,1,0:T(1,128)} %bitcast.9, f32[128,40,128]{2,1,0:T(8,128)} %all_to_all.10.in_ref), custom_call_target="tpu_custom_call" | custom-call | flops 6000000000 | bytes 12000000 | tf_op jit(solution)/shard_map/first/pallas_call | solution.py:284
  281.3 54.8 %last.1 = f32[1,1152,1152]{2,1,0:T(8,128)} custom-call(s32[16,1,1024]{2,1,0:T(1,128)} %bitcast.10, f32[128,40,128]{2,1,0:T(8,128)} %all-to-all-done.in_ref, f32[16384,128]{1,0:T(8,128)} %first.1.start_ref), custom_call_target="tpu_custom_call" | custom-call | flops 6000000000 | bytes 12000000 | tf_op jit(solution)/shard_map/last/pallas_call | solution.py:295
Async XLA Ops:
  71.0 172.1 %all-to-all-start = ((f32[128,40,128]{2,1,0:T(8,128)}), f32[128,40,128]{2,1,0:T(8,128)}, u32[]{:S(2)}, u32[]{:S(2)}) async-start(f32[128,40,128]{2,1,0:T(8,128)} %get-tuple-element.4), calls=%async_computation | async-start | bytes 5242880 | tf_op jit(solution)/shard_map/all_to_all | solution.py:257
  76.5 163.1 %all-reduce.3.cloned.1.call-start = ((), (), s32[]{:S(2)}) async-start(), calls=%async_computation.2 | async-start | bytes 393216
Sparse Core Ops, SparseCore 0:
  94.1 145.4 all-reduce.2

commit v2 on v1

--- a/solution.py
+++ b/solution.py
@@ -24,7 +24,7 @@
 
 
 def inverse_of(pt_ref, damp_ref):
-    jp = [[[pt_ref[:, 6 * o + 3 * r + k, :] for k in range(3)] for r in range(2)] for o in range(2)]
+    jp = [[[pt_ref[6 * o + 3 * r + k] for k in range(3)] for r in range(2)] for o in range(2)]
     damp = damp_ref[...]
 
     def entry(a, b):
@@ -49,15 +49,47 @@
     return home_ref[side // NBR] * NBR + side % NBR
 
 
-def pack_kernel(bp_ref, ps_ref, home_ref, cam_ref, pt_ref, damp_ref, cams_ref, out0_ref, out1_ref, mix_ref, seen_ref):
-    blocks = cam_ref.shape[0]
-    out0_ref[...] = jnp.zeros_like(out0_ref)
-    out1_ref[...] = jnp.zeros_like(out1_ref)
+def pack_kernel(which, *refs):
+    bp_ref, ps_ref, home_ref, cam_ref, pt_ref, damp_ref, cams_ref = refs[:7]
+    share_ref = refs[7] if which else None
+    out_ref, rows_ref, turned_ref, seen_ref = refs[-4:]
+    blocks = damp_ref.shape[0]
+    out_ref[...] = jnp.zeros_like(out_ref)
+    if which:
+        out_ref[:, 38:40, :] = share_ref[...]
     jp, inv = inverse_of(pt_ref, damp_ref)
+    mix = []
     for r in range(2):
         left = [sum(jp[0][r][k] * inv[k][m] for k in range(3)) for m in range(3)]
+        mix.append([-sum(left[m] * jp[1][q][m] for m in range(3)) for q in range(2)])
+
+    def put(row, value):
+        rows_ref[pl.ds(row, blocks, stride=BLK), :] = value
+
+    def turn(row, value):
+        turned_ref[pl.ds(row, blocks, stride=8), :] = value
+
+    for i in range(9):
+        row0, row1 = cam_ref[i], cam_ref[9 + i]
         for q in range(2):
-            mix_ref[2 * r + q] = -sum(left[m] * jp[1][q][m] for m in range(3))
+            mixed = row0 * mix[0][q] + row1 * mix[1][q]
+            other = cam_ref[18 + 9 * q + i]
+            if i < 8:
+                put(8 * q + i, mixed)
+                put(16 + 8 * q + i, other)
+            else:
+                put(32 + q, mixed)
+                put(34 + q, other)
+                turn(2 + q, mixed)
+                turn(q, other)
+    zero = jnp.zeros((blocks, PTS), jnp.float32)
+    for o in range(2):
+        ids = cams_ref[:, o, :].astype(jnp.float32)
+        put(36 + o, ids)
+        turn(5 - o, ids)
+        put(38 + o, zero)
+        turn(6 + o, zero)
+    tops = 38 if which else BLK
 
     def clear(i, carry):
         seen_ref[i] = 0
@@ -66,64 +98,44 @@
     lax.fori_loop(0, seen_ref.shape[0], clear, 0)
 
     def one(t, carry):
-        pair = bp_ref[t, 0]
+        pair = bp_ref[t]
         rank = seen_ref[pair]
         seen_ref[pair] = rank + 1
-        first, second = slot_of(ps_ref[pair, 0], home_ref), slot_of(ps_ref[pair, 1], home_ref)
-        row0, row1 = cam_ref[t, 0:9, :], cam_ref[t, 9:18, :]
-        other = [cam_ref[t, 18:27, :], cam_ref[t, 27:36, :]]
-        mix = [mix_ref[k, pl.ds(t, 1), :] for k in range(4)]
-        mixed = [row0 * mix[q] + row1 * mix[2 + q] for q in range(2)]
-        ids = cams_ref[t].astype(jnp.float32)
-
-        def put(out_ref, slot, a, b, ca, cb):
-            out_ref[slot, 0:8, :] = a[0][0:8]
-            out_ref[slot, 8:16, :] = a[1][0:8]
-            out_ref[slot, 16:24, :] = b[0][0:8]
-            out_ref[slot, 24:32, :] = b[1][0:8]
-            out_ref[slot, 32:33, :] = a[0][8:9]
-            out_ref[slot, 33:34, :] = a[1][8:9]
-            out_ref[slot, 34:35, :] = b[0][8:9]
-            out_ref[slot, 35:36, :] = b[1][8:9]
-            out_ref[slot, 36:37, :] = ca
-            out_ref[slot, 37:38, :] = cb
-
-        def both(out_ref):
-            put(out_ref, first, mixed, other, ids[0:1], ids[1:2])
-            put(out_ref, second, other, mixed, ids[1:2], ids[0:1])
-
-        @pl.when(rank == 0)
+
+        @pl.when(rank == which)
         def _():
-            both(out0_ref)
-
-        @pl.when(rank != 0)
-        def _():
-            both(out1_ref)
+            first, second = slot_of(ps_ref[0, pair], home_ref), slot_of(ps_ref[1, pair], home_ref)
+            base = pl.multiple_of(t * BLK, 8)
+            out_ref[first, 0:tops, :] = rows_ref[pl.ds(base, tops), :]
+            out_ref[second, 0:16, :] = rows_ref[pl.ds(base + 16, 16), :]
+            out_ref[second, 16:32, :] = rows_ref[pl.ds(base, 16), :]
+            out_ref[second, 32:tops, :] = turned_ref[pl.ds(pl.multiple_of(t * 8, 8), tops - 32), :]
 
         return carry
 
     lax.fori_loop(0, blocks, one, 0)
 
 
-def rhs_kernel(bp_ref, ps_ref, home_ref, cam_ref, pt_ref, res_ref, damp_ref, cams_ref, out_ref, w_ref):
-    blocks = cam_ref.shape[0]
+def rhs_kernel(bp_ref, ps_ref, home_ref, cam_ref, pt_ref, res_ref, damp_ref, cams_ref, out_ref, b_ref):
+    blocks = damp_ref.shape[0]
     out_ref[...] = jnp.zeros_like(out_ref)
+    b_ref[...] = jnp.zeros_like(b_ref)
     jp, inv = inverse_of(pt_ref, damp_ref)
     err = [[res_ref[:, 2 * o + r, :] for r in range(2)] for o in range(2)]
     gp = [sum(jp[o][r][k] * err[o][r] for o in range(2) for r in range(2)) for k in range(3)]
     z = [sum(inv[k][m] * gp[m] for m in range(3)) for k in range(3)]
     for o in range(2):
-        for r in range(2):
-            w_ref[2 * o + r] = err[o][r] - sum(jp[o][r][k] * z[k] for k in range(3))
+        w = [err[o][r] - sum(jp[o][r][k] * z[k] for k in range(3)) for r in range(2)]
+        for i in range(9):
+            value = cam_ref[18 * o + i] * w[0] + cam_ref[18 * o + 9 + i] * w[1]
+            b_ref[pl.ds(16 * o + i, blocks, stride=32), :] = value
     number = lax.broadcasted_iota(jnp.int32, (CAMS, PTS), 0)
 
     def one(t, carry):
-        pair = bp_ref[t, 0]
+        pair = bp_ref[t]
         for o in range(2):
-            home = home_ref[ps_ref[pair, o] // NBR]
-            b = cam_ref[t, 18 * o : 18 * o + 9, :] * w_ref[2 * o, pl.ds(t, 1), :]
-            b = b + cam_ref[t, 18 * o + 9 : 18 * o + 18, :] * w_ref[2 * o + 1, pl.ds(t, 1), :]
-            b = jnp.concatenate([b, jnp.zeros((7, PTS), jnp.float32)], axis=0)
+            home = home_ref[ps_ref[o, pair] // NBR]
+            b = b_ref[pl.ds(pl.multiple_of(t * 32, 32) + 16 * o, 16), :]
             high = b.astype(jnp.bfloat16)
             low = (b - high.astype(jnp.float32)).astype(jnp.bfloat16)
             hit = jnp.where(number == cams_ref[t, o : o + 1, :], 1.0, 0.0).astype(jnp.bfloat16)
@@ -133,7 +145,7 @@
             out_ref[home] = out_ref[home] + (added[0:16] + added[16:32])
         return carry
 
-    lax.fori_loop(0, blocks, one, 0)
+    lax.fori_loop(0, blocks, one, 0, unroll=4)
 
 
 def expand(block):
@@ -243,35 +255,47 @@
     smem = pl.BlockSpec(memory_space=pltpu.SMEM)
     vmem = pl.BlockSpec(memory_space=pltpu.VMEM)
     blocks = cam_jac.shape[0]
-    sent = jax.ShapeDtypeStruct((SIDES, BLK, PTS), jnp.float32)
-    out0, out1 = pl.pallas_call(
-        pack_kernel,
-        in_specs=[smem] * 3 + [vmem] * 4,
-        out_specs=[vmem, vmem],
-        out_shape=[sent, sent],
-        scratch_shapes=[pltpu.VMEM((4, blocks, PTS), jnp.float32), pltpu.SMEM((pair_sides.shape[0],), jnp.int32)],
-        compiler_params=params(),
-        name="pack",
-    )(block_pair, pair_sides, cluster_home, cam_jac, pt_jac, damping, cams)
-    in0 = lax.all_to_all(out0, RC, 0, 0, tiled=True)
-    in1 = lax.all_to_all(out1, RC, 0, 0, tiled=True)
+    rows, cols = lax.axis_size("row"), lax.axis_size("col")
+    tables = (block_pair.reshape(-1), pair_sides.T, cluster_home)
+    cam_rows, pt_rows = jnp.transpose(cam_jac, (1, 0, 2)), jnp.transpose(pt_jac, (1, 0, 2))
+
+    def pack(which, *shares):
+        return pl.pallas_call(
+            functools.partial(pack_kernel, which),
+            in_specs=[smem] * 3 + [vmem] * (4 + len(shares)),
+            out_specs=vmem,
+            out_shape=jax.ShapeDtypeStruct((SIDES, BLK, PTS), jnp.float32),
+            scratch_shapes=[
+                pltpu.VMEM((blocks * BLK, PTS), jnp.float32),
+                pltpu.VMEM((blocks * 8, PTS), jnp.float32),
+                pltpu.SMEM((pair_sides.shape[0],), jnp.int32),
+            ],
+            compiler_params=params(),
+            cost_estimate=pl.CostEstimate(flops=10**7, bytes_accessed=6 * 10**6, transcendentals=0),
+            name="pack" + str(which),
+        )(*tables, cam_rows, pt_rows, damping, cams, *shares)
+
+    in0 = lax.all_to_all(pack(0), RC, 0, 0, tiled=True)
 
     partial = pl.pallas_call(
         rhs_kernel,
         in_specs=[smem] * 3 + [vmem] * 5,
         out_specs=vmem,
         out_shape=jax.ShapeDtypeStruct((CLUSTERS, 16, CAMS), jnp.float32),
-        scratch_shapes=[pltpu.VMEM((4, blocks, PTS), jnp.float32)],
+        scratch_shapes=[pltpu.VMEM((blocks * 32, PTS), jnp.float32)],
         compiler_params=params(),
-        cost_estimate=pl.CostEstimate(flops=10**8, bytes_accessed=3 * 10**6, transcendentals=0),
+        cost_estimate=pl.CostEstimate(flops=10**10, bytes_accessed=3 * 10**6, transcendentals=0),
         name="rhs",
-    )(block_pair, pair_sides, cluster_home, cam_jac, pt_jac, resid, damping, cams)
-    rows, cols = lax.axis_size("row"), lax.axis_size("col")
-    shares = partial[:, 0:9].reshape(rows, CLUSTERS // rows, 9, cols, CAMS // cols)
-    shares = jnp.transpose(shares, (0, 3, 1, 2, 4)).reshape(rows * cols, -1)
-    share = lax.psum_scatter(shares, RC, scatter_dimension=0, tiled=True)
-    share = share.reshape(CLUSTERS // rows, 9, CAMS // cols)
-    reduced_rhs = jnp.transpose(share, (0, 2, 1)).reshape(CLUSTERS // rows, WIDTH // cols)
+    )(*tables, cam_rows, pt_rows, resid, damping, cams)
+    halves = partial.reshape(rows, CLUSTERS // rows, 16, CAMS)
+    core = lax.axis_index("col") % 2
+    mine = lax.dynamic_index_in_dim(halves, core, 1, keepdims=False)
+    other = lax.dynamic_index_in_dim(halves, 1 - core, 1, keepdims=False)
+    mine = mine + lax.ppermute(other, "col", [(c, c ^ 1) for c in range(cols)])
+    shares = jnp.transpose(mine.reshape(rows, 16, cols, CAMS // cols), (0, 2, 1, 3))
+    in1 = lax.all_to_all(pack(1, shares.reshape(SIDES, 2, PTS)), RC, 0, 0, tiled=True)
+    share = jnp.sum(in1[:, 38:40, :].reshape(SIDES // 2, 2, 2, PTS), axis=0).reshape(2, 16, CAMS // cols)
+    reduced_rhs = jnp.transpose(share[:, 0:9], (0, 2, 1)).reshape(2, WIDTH // cols)
 
     steps = SIDES // GROUP
     cells = CAMS * CAMS

time: 344 us -> 154 us (0.45)
  waiting for transfers between devices: 146 us -> 18.7 us
  blocking collectives: 47.7 us -> 0 us
  between operations: 14.1 us -> 0.7 us
  starting transfers between devices: 5.72 us -> 17.6 us
  local copies, waits for them, and re-layouts: 12.8 us -> 3.71 us
  Pallas kernels: 113 us -> 109 us
    unnamed x2 -> x0, waiting for transfers between devices: 146 us -> none
    all_to_all x1 -> x0, blocking collectives: 47.7 us -> none  [local(): in0 = lax.all_to_all(out0, RC, 0, 0, tiled=True)]
    all_to_all x1 -> x2, waiting for transfers between devices: 0.01 us -> 17.8 us  [the longest x1 17.8 us: local(): in0 = lax.all_to_all(pack(0), RC, 0, 0, tiled=True)]
    all_to_all x1 -> x2, starting transfers between devices: 5.5 us -> 16.4 us  [the longest x1 11.9 us: local(): in0 = lax.all_to_all(pack(0), RC, 0, 0, tiled=True)]
    unnamed x5 -> x2, local copies, waits for them, and re-layouts: 8.54 us -> 0.01 us
    pallas_call x1, Pallas kernels: 13.8 us -> 7.11 us  [local(): pl.pallas_call(rhs_kernel, in_specs=[smem] * 3 + [vmem] * 5, out_specs=vm...]
    pallas_call x1 -> x2, Pallas kernels: 8.35 us -> 11.4 us  [pack(): pl.pallas_call(functools.partial(pack_kernel, which), in_specs=[smem] * 3...]
  transfers between devices with their start and end apart: 2 -> 3, of which waited for: 1 -> 2; matrix products, arithmetic and copies ran while one was open for 2% -> 4% of each run, Pallas kernels for 4% -> 31%
where the time goes in v2:
time: 154 us
  Pallas kernels  109 us (71%)
  waiting for transfers between devices  18.7 us (12%)
  starting transfers between devices  17.6 us (11%)
  other arithmetic  3.79 us (2%)
  local copies, waits for them, and re-layouts  3.71 us (2%)
    pallas_call x1, Pallas kernels, local(): pl.pallas_call(functools.partial(last_kernel, steps), grid=(steps + CAMS...  54.8 us
    pallas_call x1, Pallas kernels, local(): pl.pallas_call(functools.partial(first_kernel, steps), grid=(steps + cell...  36.1 us
    all_to_all x1, waiting for transfers between devices, local(): in0 = lax.all_to_all(pack(0), RC, 0, 0, tiled=True)  17.8 us
    all_to_all x1, starting transfers between devices, local(): in0 = lax.all_to_all(pack(0), RC, 0, 0, tiled=True)  11.9 us
    pallas_call x2, Pallas kernels, pack(): pl.pallas_call(functools.partial(pack_kernel, which), in_specs=[smem] * 3...  11.4 us
    pallas_call x1, Pallas kernels, local(): pl.pallas_call(rhs_kernel, in_specs=[smem] * 3 + [vmem] * 5, out_specs=vm...  7.11 us
    all_to_all x1, starting transfers between devices, local(): lax.all_to_all(pack(1, shares.reshape(SIDES, 2, PTS)), RC, 0, 0, tiled=True)  4.5 us
  transfers between devices with their start and end apart: 3, of which 2 were waited for; matrix products, arithmetic and copies ran while one was open for 4% of the time, Pallas kernels for 31%

profile of v2, /device:TPU:1, one launch (start us, length us, event | category | flops | bytes accessed | tf_op | source)
XLA Modules:
  0.0 154.0 jit_solution(8427441893364051022)
XLA Ops:
  0.6 6.1 %pack0.1 = f32[128,40,128]{2,1,0:T(8,128)} custom-call(s32[64]{0:T(128)} %bitcast.32, s32[2,64]{1,0:T(2,128)} %bitcast.29, s32[32]{0:T(128)} %refs_2_.3, f32[36,64,128]{2,1,0:T(8,128)} %bitcast.17, f32[12,64,128]{2,1,0:T(8,128)} %bitcast.21, f32[64,128]{1,0:T(8,128)} %refs_5_.3, s32[64,2,128]{2,1,0:T(2,128)} %refs_6_.3), custom_call_target="tpu_custom_call" | custom-call | flops 10000000 | bytes 6000000 | tf_op jit(solution)/shard_map/pack0/pallas_call | solution.py:263
  6.7 11.9 %all-to-all-start.1 = ((f32[128,40,128]{2,1,0:T(8,128)}), f32[128,40,128]{2,1,0:T(8,128)}, u32[]{:S(2)}, u32[]{:S(2)}) async-start(f32[128,40,128]{2,1,0:T(8,128)} %pack0.1), calls=%async_computation.1 | async-start | bytes 5242880 | tf_op jit(solution)/shard_map/all_to_all | solution.py:278
  18.7 7.1 %rhs.1 = f32[32,16,128]{2,1,0:T(8,128)} custom-call(s32[64]{0:T(128)} %bitcast.33, s32[2,64]{1,0:T(2,128)} %bitcast.30, s32[32]{0:T(128)} %refs_2_.3, f32[36,64,128]{2,1,0:T(8,128)} %bitcast.18, f32[12,64,128]{2,1,0:T(8,128)} %bitcast.22, f32[64,4,128]{2,1,0:T(4,128)} %res_ref.1, f32[64,128]{1,0:T(8,128)} %refs_5_.3, s32[64,2,128]{2,1,0:T(2,128)} %refs_6_.3), custom_call_target="tpu_custom_call" | custom-call | flops 10000000000 | bytes 3000000 | tf_op jit(solution)/shard_map/rhs/pallas_call | solution.py:280
  25.8 0.9 dynamic-slice_bitcast_fusion
  26.7 1.2 collective-permute-start
  27.9 1.0 collective-permute-done
  28.9 0.9 bitcast_add_fusion
  29.8 0.3 reshape.83
  30.1 0.2 copy.12
  30.3 1.1 reshape.84.refs_7_
  31.4 5.3 %pack1.1 = f32[128,40,128]{2,1,0:T(8,128)} custom-call(s32[64]{0:T(128)} %bitcast.34, s32[2,64]{1,0:T(2,128)} %bitcast.31, s32[32]{0:T(128)} %refs_2_.3, f32[36,64,128]{2,1,0:T(8,128)} %bitcast.19, f32[12,64,128]{2,1,0:T(8,128)} %bitcast.23, f32[64,128]{1,0:T(8,128)} %refs_5_.3, s32[64,2,128]{2,1,0:T(2,128)} %refs_6_.3, f32[128,2,128]{2,1,0:T(2,128)} %reshape.84.refs_7_), custom_call_target="tpu_custom_call" | custom-call | flops 10000000 | bytes 6000000 | tf_op jit(solution)/shard_map/pack1/pallas_call | solution.py:263
  36.7 17.8 %all-to-all-done.1.in_ref = f32[128,40,128]{2,1,0:T(8,128)} async-done(((f32[128,40,128]{2,1,0:T(8,128)}), f32[128,40,128]{2,1,0:T(8,128)}, u32[]{:S(2)}, u32[]{:S(2)}) %all-to-all-start.1) | async-done | bytes 2621472 | tf_op jit(solution)/shard_map/all_to_all | solution.py:278
  54.4 4.5 %all-to-all-start = ((f32[128,40,128]{2,1,0:T(8,128)}), f32[128,40,128]{2,1,0:T(8,128)S(1)}, u32[]{:S(2)}, u32[]{:S(2)}) async-start(f32[128,40,128]{2,1,0:T(8,128)} %pack1.1), calls=%async_computation | async-start | bytes 5242880 | tf_op jit(solution)/shard_map/all_to_all | solution.py:296
  59.0 2.0 %fusion = s32[128,1,128]{2,1,0:T(1,128)} fusion(f32[128,40,128]{2,1,0:T(8,128)} %all-to-all-done.1.in_ref), kind=kLoop, calls=%fused_computation.3 | loop fusion | flops 49152 | bytes 196608 | tf_op jit(solution)/shard_map/convert_element_type | solution.py:251
  61.0 36.1 %first.1.start_ref = f32[16384,128]{1,0:T(8,128)} custom-call(s32[16,1,1024]{2,1,0:T(1,128)} %bitcast.28, f32[128,40,128]{2,1,0:T(8,128)} %all-to-all-done.1.in_ref), custom_call_target="tpu_custom_call" | custom-call | flops 6000000000 | bytes 12000000 | tf_op jit(solution)/shard_map/first/pallas_call | solution.py:308
  97.1 0.0 all-to-all-done.in_ref
  97.1 0.0 copy-start
  97.1 0.1 slice.28
  97.2 0.1 reduce_sum.9
  97.2 0.1 reshape.86
  97.3 0.1 copy.15
  97.4 1.0 reshape.87
  98.4 0.8 fusion.1
  99.2 0.0 copy-done
  99.2 54.8 %last.1 = f32[1,1152,1152]{2,1,0:T(8,128)} custom-call(s32[16,1,1024]{2,1,0:T(1,128)} %bitcast.27, f32[128,40,128]{2,1,0:T(8,128)} %copy-done, f32[16384,128]{1,0:T(8,128)} %first.1.start_ref), custom_call_target="tpu_custom_call" | custom-call | flops 6000000000 | bytes 12000000 | tf_op jit(solution)/shard_map/last/pallas_call | solution.py:319
  (1 shorter events, 0.0 us)
Async XLA Ops:
  6.7 47.7 %all-to-all-start.1 = ((f32[128,40,128]{2,1,0:T(8,128)}), f32[128,40,128]{2,1,0:T(8,128)}, u32[]{:S(2)}, u32[]{:S(2)}) async-start(f32[128,40,128]{2,1,0:T(8,128)} %pack0.1), calls=%async_computation.1 | async-start | bytes 5242880 | tf_op jit(solution)/shard_map/all_to_all | solution.py:278
  26.7 2.2 %collective-permute-start = (f32[16,16,128]{2,1,0:T(8,128)S(1)}, f32[16,16,128]{2,1,0:T(8,128)S(1)}, u32[]{:S(2)}, u32[]{:S(2)}) collective-permute-start(f32[16,16,128]{2,1,0:T(8,128)S(1)} %dynamic-slice_bitcast_fusion), channel_id=1, source_target_pairs={{0,1},{1,0},{2,3},{3,2},{4,5},{5,4},{6,7},{7,6},{8,9},{9,8},{10,11... | collective-permute-start | bytes 393224 | tf_op jit(solution)/shard_map/ppermute | solution.py:294
  54.4 42.6 %all-to-all-start = ((f32[128,40,128]{2,1,0:T(8,128)}), f32[128,40,128]{2,1,0:T(8,128)S(1)}, u32[]{:S(2)}, u32[]{:S(2)}) async-start(f32[128,40,128]{2,1,0:T(8,128)} %pack1.1), calls=%async_computation | async-start | bytes 5242880 | tf_op jit(solution)/shard_map/all_to_all | solution.py:296
  97.1 2.1 %copy-start = (f32[128,40,128]{2,1,0:T(8,128)}, f32[128,40,128]{2,1,0:T(8,128)S(1)}, u32[]{:S(2)}) copy-start(f32[128,40,128]{2,1,0:T(8,128)S(1)} %all-to-all-done.in_ref) | copy-start | bytes 7864324

commit v3 on v2

--- a/solution.py
+++ b/solution.py
@@ -14,10 +14,9 @@
 SIDES = 128
 CLUSTERS = 32
 BLK = 40
-GROUP = 8
+GROUP = 16
 TABLES = 4
-UNROLL = 32
-FINAL = 8
+FINAL = 16
 FEATS = 88
 VMEM_LIMIT = 60 * 2**20
 RC = ("row", "col")
@@ -54,7 +53,10 @@
     share_ref = refs[7] if which else None
     out_ref, rows_ref, turned_ref, seen_ref = refs[-4:]
     blocks = damp_ref.shape[0]
-    out_ref[...] = jnp.zeros_like(out_ref)
+    out_ref[:, 0:36, :] = jnp.zeros((SIDES, 36, PTS), jnp.float32)
+    spots = lax.broadcasted_iota(jnp.int32, (SIDES, 4, PTS), 2)
+    spots = jnp.where(lax.broadcasted_iota(jnp.int32, (SIDES, 4, PTS), 1) < 2, spots, 0)
+    out_ref[:, 36:40, :] = spots.astype(jnp.float32)
     if which:
         out_ref[:, 38:40, :] = share_ref[...]
     jp, inv = inverse_of(pt_ref, damp_ref)
@@ -159,20 +161,19 @@
 
 
 def accumulate(idx_ref, in_ref, pay_ref, tabs):
-    for g in range(GROUP):
+    def widen(g):
         rows = expand(in_ref[g])
         rows.append(jnp.zeros((CAMS - FEATS, PTS), jnp.float32))
-        pay_ref[pl.ds(g * PTS, PTS), :] = jnp.concatenate(rows, axis=0).T
-
-    def body(q, carry):
-        base = pl.multiple_of(q * UNROLL, UNROLL)
-        for u in range(UNROLL):
-            i = idx_ref[0, 0, base + u]
+        pay_ref[g * PTS : (g + 1) * PTS, :] = jnp.concatenate(rows, axis=0).T
+
+    widen(0)
+    for g in range(GROUP):
+        if g + 1 < GROUP:
+            widen(g + 1)
+        for u in range(g * PTS, (g + 1) * PTS):
+            i = idx_ref[0, 0, u]
             tab = tabs[u % TABLES]
-            tab[pl.ds(i, 1), :] = tab[pl.ds(i, 1), :] + pay_ref[pl.ds(base + u, 1), :]
-        return carry
-
-    lax.fori_loop(0, GROUP * PTS // UNROLL, body, 0)
+            tab[pl.ds(i, 1), :] = tab[pl.ds(i, 1), :] + pay_ref[u : u + 1, :]
 
 
 def first_kernel(steps, idx_ref, in_ref, out_ref, pay_ref, *tabs):
@@ -251,6 +252,44 @@
     return cell.astype(jnp.int32).reshape(SIDES // GROUP, 1, GROUP * PTS)
 
 
+def schur(in0, in1):
+    steps = SIDES // GROUP
+    cells = CAMS * CAMS
+    part = 4096
+    spec_idx = pl.BlockSpec((1, 1, GROUP * PTS), lambda s: (jnp.minimum(s, steps - 1), 0, 0), memory_space=pltpu.SMEM)
+    spec_in = pl.BlockSpec((GROUP, BLK, PTS), lambda s: (jnp.minimum(s, steps - 1), 0, 0))
+    tabs = [pltpu.VMEM((cells, PTS), jnp.float32)] * TABLES
+    pay = pltpu.VMEM((GROUP * PTS, PTS), jnp.float32)
+    cost = pl.CostEstimate(flops=6 * 10**9, bytes_accessed=12 * 10**6, transcendentals=0)
+    total = pl.pallas_call(
+        functools.partial(first_kernel, steps),
+        grid=(steps + cells // part,),
+        in_specs=[spec_idx, spec_in],
+        out_specs=pl.BlockSpec((part, PTS), lambda s: (jnp.maximum(s - steps, 0), 0)),
+        out_shape=jax.ShapeDtypeStruct((cells, PTS), jnp.float32),
+        scratch_shapes=[pay] + tabs,
+        compiler_params=params(),
+        cost_estimate=cost,
+        name="first",
+    )(index_of(in0), in0)
+    return pl.pallas_call(
+        functools.partial(last_kernel, steps),
+        grid=(steps + CAMS // FINAL,),
+        in_specs=[spec_idx, spec_in, pl.BlockSpec(memory_space=pltpu.VMEM)],
+        out_specs=pl.BlockSpec((1, 9 * FINAL, WIDTH), lambda s: (0, jnp.maximum(s - steps, 0), 0)),
+        out_shape=jax.ShapeDtypeStruct((1, WIDTH, WIDTH), jnp.float32),
+        scratch_shapes=[
+            pay,
+            pltpu.VMEM((2 * CAMS, WIDTH), jnp.bfloat16),
+            pltpu.VMEM((FINAL * FEATS, WIDTH), jnp.float32),
+        ]
+        + tabs,
+        compiler_params=params(),
+        cost_estimate=cost,
+        name="last",
+    )(index_of(in1), in1, total)
+
+
 def local(cam_jac, pt_jac, resid, damping, cams, block_pair, pair_sides, cluster_home):
     smem = pl.BlockSpec(memory_space=pltpu.SMEM)
     vmem = pl.BlockSpec(memory_space=pltpu.VMEM)
@@ -297,42 +336,7 @@
     share = jnp.sum(in1[:, 38:40, :].reshape(SIDES // 2, 2, 2, PTS), axis=0).reshape(2, 16, CAMS // cols)
     reduced_rhs = jnp.transpose(share[:, 0:9], (0, 2, 1)).reshape(2, WIDTH // cols)
 
-    steps = SIDES // GROUP
-    cells = CAMS * CAMS
-    part = 2048
-    spec_idx = pl.BlockSpec((1, 1, GROUP * PTS), lambda s: (jnp.minimum(s, steps - 1), 0, 0), memory_space=pltpu.SMEM)
-    spec_in = pl.BlockSpec((GROUP, BLK, PTS), lambda s: (jnp.minimum(s, steps - 1), 0, 0))
-    tabs = [pltpu.VMEM((cells, PTS), jnp.float32)] * TABLES
-    pay = pltpu.VMEM((GROUP * PTS, PTS), jnp.float32)
-    cost = pl.CostEstimate(flops=6 * 10**9, bytes_accessed=12 * 10**6, transcendentals=0)
-    total = pl.pallas_call(
-        functools.partial(first_kernel, steps),
-        grid=(steps + cells // part,),
-        in_specs=[spec_idx, spec_in],
-        out_specs=pl.BlockSpec((part, PTS), lambda s: (jnp.maximum(s - steps, 0), 0)),
-        out_shape=jax.ShapeDtypeStruct((cells, PTS), jnp.float32),
-        scratch_shapes=[pay] + tabs,
-        compiler_params=params(),
-        cost_estimate=cost,
-        name="first",
-    )(index_of(in0), in0)
-    schur = pl.pallas_call(
-        functools.partial(last_kernel, steps),
-        grid=(steps + CAMS // FINAL,),
-        in_specs=[spec_idx, spec_in, vmem],
-        out_specs=pl.BlockSpec((1, 9 * FINAL, WIDTH), lambda s: (0, jnp.maximum(s - steps, 0), 0)),
-        out_shape=jax.ShapeDtypeStruct((1, WIDTH, WIDTH), jnp.float32),
-        scratch_shapes=[
-            pay,
-            pltpu.VMEM((2 * CAMS, WIDTH), jnp.bfloat16),
-            pltpu.VMEM((FINAL * FEATS, WIDTH), jnp.float32),
-        ]
-        + tabs,
-        compiler_params=params(),
-        cost_estimate=cost,
-        name="last",
-    )(index_of(in1), in1, total)
-    return schur, reduced_rhs
+    return schur(in0, in1), reduced_rhs
 
 
 def solution(mesh):

time: 154 us -> 138 us (0.90)
  Pallas kernels: 109 us -> 87 us
  waiting for transfers between devices: 18.7 us -> 24.4 us
    pallas_call x2, Pallas kernels: 91 us -> 68.5 us  [the longest x1 40 us: schur(): pl.pallas_call(functools.partial(last_kernel, steps), grid=(steps + CAMS...]
    all_to_all x1, waiting for transfers between devices: 0.01 us -> 5.67 us  [local(): lax.all_to_all(pack(1, shares.reshape(SIDES, 2, PTS)), RC, 0, 0, tiled=True)]
  transfers between devices with their start and end apart: 3 -> 3, of which waited for: 2 -> 3; matrix products, arithmetic and copies ran while one was open for 4% -> 4% of each run, Pallas kernels for 31% -> 30%
where the time goes in v3:
time: 138 us; the launch traced here: 137 us
  Pallas kernels  87 us (63%)
  waiting for transfers between devices  24.4 us (18%)
  starting transfers between devices  17.6 us (13%)
  other arithmetic  3.79 us (3%)
  local copies, waits for them, and re-layouts  3.71 us (3%)
    pallas_call x1, Pallas kernels, schur(): pl.pallas_call(functools.partial(last_kernel, steps), grid=(steps + CAMS...  40 us
    pallas_call x1, Pallas kernels, schur(): pl.pallas_call(functools.partial(first_kernel, steps), grid=(steps + cell...  28.5 us
    all_to_all x1, waiting for transfers between devices, local(): in0 = lax.all_to_all(pack(0), RC, 0, 0, tiled=True)  17.7 us
    all_to_all x1, starting transfers between devices, local(): in0 = lax.all_to_all(pack(0), RC, 0, 0, tiled=True)  11.9 us
    pallas_call x2, Pallas kernels, pack(): pl.pallas_call(functools.partial(pack_kernel, which), in_specs=[smem] * 3...  11.4 us
    pallas_call x1, Pallas kernels, local(): pl.pallas_call(rhs_kernel, in_specs=[smem] * 3 + [vmem] * 5, out_specs=vm...  7.11 us
    all_to_all x1, waiting for transfers between devices, local(): lax.all_to_all(pack(1, shares.reshape(SIDES, 2, PTS)), RC, 0, 0, tiled=True)  5.67 us
    all_to_all x1, starting transfers between devices, local(): lax.all_to_all(pack(1, shares.reshape(SIDES, 2, PTS)), RC, 0, 0, tiled=True)  4.5 us
  transfers between devices with their start and end apart: 3, of which 3 were waited for; matrix products, arithmetic and copies ran while one was open for 4% of the time, Pallas kernels for 30%

profile of v3, /device:TPU:1, one launch (start us, length us, event | category | flops | bytes accessed | tf_op | source)
XLA Modules:
  0.0 137.2 jit_solution(316145127729019535)
XLA Ops:
  0.6 6.1 %pack0.1 = f32[128,40,128]{2,1,0:T(8,128)} custom-call(s32[64]{0:T(128)} %bitcast.32, s32[2,64]{1,0:T(2,128)} %bitcast.29, s32[32]{0:T(128)} %refs_2_.3, f32[36,64,128]{2,1,0:T(8,128)} %bitcast.17, f32[12,64,128]{2,1,0:T(8,128)} %bitcast.21, f32[64,128]{1,0:T(8,128)} %refs_5_.3, s32[64,2,128]{2,1,0:T(2,128)} %refs_6_.3), custom_call_target="tpu_custom_call" | custom-call | flops 10000000 | bytes 6000000 | tf_op jit(solution)/shard_map/pack0/pallas_call | solution.py:302
  6.8 11.9 %all-to-all-start.1 = ((f32[128,40,128]{2,1,0:T(8,128)}), f32[128,40,128]{2,1,0:T(8,128)}, u32[]{:S(2)}, u32[]{:S(2)}) async-start(f32[128,40,128]{2,1,0:T(8,128)} %pack0.1), calls=%async_computation.1 | async-start | bytes 5242880 | tf_op jit(solution)/shard_map/all_to_all | solution.py:317
  18.7 7.1 %rhs.1 = f32[32,16,128]{2,1,0:T(8,128)} custom-call(s32[64]{0:T(128)} %bitcast.33, s32[2,64]{1,0:T(2,128)} %bitcast.30, s32[32]{0:T(128)} %refs_2_.3, f32[36,64,128]{2,1,0:T(8,128)} %bitcast.18, f32[12,64,128]{2,1,0:T(8,128)} %bitcast.22, f32[64,4,128]{2,1,0:T(4,128)} %res_ref.1, f32[64,128]{1,0:T(8,128)} %refs_5_.3, s32[64,2,128]{2,1,0:T(2,128)} %refs_6_.3), custom_call_target="tpu_custom_call" | custom-call | flops 10000000000 | bytes 3000000 | tf_op jit(solution)/shard_map/rhs/pallas_call | solution.py:319
  25.8 0.9 dynamic-slice_bitcast_fusion
  26.7 1.2 collective-permute-start
  27.9 1.0 collective-permute-done
  28.9 0.9 bitcast_add_fusion
  29.8 0.3 reshape.83
  30.1 0.2 copy.12
  30.3 1.1 reshape.84.refs_7_
  31.4 5.3 %pack1.1 = f32[128,40,128]{2,1,0:T(8,128)} custom-call(s32[64]{0:T(128)} %bitcast.34, s32[2,64]{1,0:T(2,128)} %bitcast.31, s32[32]{0:T(128)} %refs_2_.3, f32[36,64,128]{2,1,0:T(8,128)} %bitcast.19, f32[12,64,128]{2,1,0:T(8,128)} %bitcast.23, f32[64,128]{1,0:T(8,128)} %refs_5_.3, s32[64,2,128]{2,1,0:T(2,128)} %refs_6_.3, f32[128,2,128]{2,1,0:T(2,128)} %reshape.84.refs_7_), custom_call_target="tpu_custom_call" | custom-call | flops 10000000 | bytes 6000000 | tf_op jit(solution)/shard_map/pack1/pallas_call | solution.py:302
  36.7 17.7 %all-to-all-done.1.in_ref = f32[128,40,128]{2,1,0:T(8,128)} async-done(((f32[128,40,128]{2,1,0:T(8,128)}), f32[128,40,128]{2,1,0:T(8,128)}, u32[]{:S(2)}, u32[]{:S(2)}) %all-to-all-start.1) | async-done | bytes 2621472 | tf_op jit(solution)/shard_map/all_to_all | solution.py:317
  54.5 4.5 %all-to-all-start = ((f32[128,40,128]{2,1,0:T(8,128)}), f32[128,40,128]{2,1,0:T(8,128)S(1)}, u32[]{:S(2)}, u32[]{:S(2)}) async-start(f32[128,40,128]{2,1,0:T(8,128)} %pack1.1), calls=%async_computation | async-start | bytes 5242880 | tf_op jit(solution)/shard_map/all_to_all | solution.py:335
  59.0 2.0 %fusion = s32[128,1,128]{2,1,0:T(1,128)} fusion(f32[128,40,128]{2,1,0:T(8,128)} %all-to-all-done.1.in_ref), kind=kLoop, calls=%fused_computation.3 | loop fusion | flops 49152 | bytes 196608 | tf_op jit(solution)/shard_map/convert_element_type | solution.py:252
  61.0 28.5 %first.1.start_ref = f32[16384,128]{1,0:T(8,128)} custom-call(s32[8,1,2048]{2,1,0:T(1,128)} %bitcast.28, f32[128,40,128]{2,1,0:T(8,128)} %all-to-all-done.1.in_ref), custom_call_target="tpu_custom_call" | custom-call | flops 6000000000 | bytes 12000000 | tf_op jit(solution)/shard_map/first/pallas_call | solution.py:264
  89.5 5.7 %all-to-all-done.in_ref = f32[128,40,128]{2,1,0:T(8,128)S(1)} async-done(((f32[128,40,128]{2,1,0:T(8,128)}), f32[128,40,128]{2,1,0:T(8,128)S(1)}, u32[]{:S(2)}, u32[]{:S(2)}) %all-to-all-start) | async-done | bytes 2621472 | tf_op jit(solution)/shard_map/all_to_all | solution.py:335
  95.2 0.0 copy-start
  95.2 0.1 slice.28
  95.3 0.1 reduce_sum.9
  95.4 0.1 reshape.86
  95.4 0.1 copy.15
  95.5 1.0 reshape.87
  96.5 0.8 fusion.1
  97.3 0.0 copy-done
  97.3 40.0 %last.1 = f32[1,1152,1152]{2,1,0:T(8,128)} custom-call(s32[8,1,2048]{2,1,0:T(1,128)} %bitcast.27, f32[128,40,128]{2,1,0:T(8,128)} %copy-done, f32[16384,128]{1,0:T(8,128)} %first.1.start_ref), custom_call_target="tpu_custom_call" | custom-call | flops 6000000000 | bytes 12000000 | tf_op jit(solution)/shard_map/last/pallas_call | solution.py:275
  (1 shorter events, 0.0 us)
Async XLA Ops:
  6.8 47.7 %all-to-all-start.1 = ((f32[128,40,128]{2,1,0:T(8,128)}), f32[128,40,128]{2,1,0:T(8,128)}, u32[]{:S(2)}, u32[]{:S(2)}) async-start(f32[128,40,128]{2,1,0:T(8,128)} %pack0.1), calls=%async_computation.1 | async-start | bytes 5242880 | tf_op jit(solution)/shard_map/all_to_all | solution.py:317
  26.7 2.2 %collective-permute-start = (f32[16,16,128]{2,1,0:T(8,128)S(1)}, f32[16,16,128]{2,1,0:T(8,128)S(1)}, u32[]{:S(2)}, u32[]{:S(2)}) collective-permute-start(f32[16,16,128]{2,1,0:T(8,128)S(1)} %dynamic-slice_bitcast_fusion), channel_id=1, source_target_pairs={{0,1},{1,0},{2,3},{3,2},{4,5},{5,4},{6,7},{7,6},{8,9},{9,8},{10,11... | collective-permute-start | bytes 393224 | tf_op jit(solution)/shard_map/ppermute | solution.py:333
  54.5 40.7 %all-to-all-start = ((f32[128,40,128]{2,1,0:T(8,128)}), f32[128,40,128]{2,1,0:T(8,128)S(1)}, u32[]{:S(2)}, u32[]{:S(2)}) async-start(f32[128,40,128]{2,1,0:T(8,128)} %pack1.1), calls=%async_computation | async-start | bytes 5242880 | tf_op jit(solution)/shard_map/all_to_all | solution.py:335
  95.2 2.1 %copy-start = (f32[128,40,128]{2,1,0:T(8,128)}, f32[128,40,128]{2,1,0:T(8,128)S(1)}, u32[]{:S(2)}) copy-start(f32[128,40,128]{2,1,0:T(8,128)S(1)} %all-to-all-done.in_ref) | copy-start | bytes 7864324

commit v4 on v3

--- a/solution.py
+++ b/solution.py
@@ -15,10 +15,10 @@
 CLUSTERS = 32
 BLK = 40
 GROUP = 16
-TABLES = 4
+TABLES = 6
 FINAL = 16
 FEATS = 88
-VMEM_LIMIT = 60 * 2**20
+VMEM_LIMIT = 62 * 2**20
 RC = ("row", "col")
 
 
@@ -160,34 +160,56 @@
     return rows
 
 
-def accumulate(idx_ref, in_ref, pay_ref, tabs):
+def fetch(idx_hbm, ids, sem, step, half):
+    return pltpu.make_async_copy(idx_hbm.at[2 * step + half], ids[half], sem.at[half])
+
+
+def accumulate(step, steps, idx_hbm, in_ref, pay_ref, ids, sem, tabs):
     def widen(g):
         rows = expand(in_ref[g])
         rows.append(jnp.zeros((CAMS - FEATS, PTS), jnp.float32))
         pay_ref[g * PTS : (g + 1) * PTS, :] = jnp.concatenate(rows, axis=0).T
 
+    later = jnp.minimum(step + 1, steps - 1)
     widen(0)
     for g in range(GROUP):
+        half, place = divmod(g, GROUP // 2)
+        if place == 0:
+            fetch(idx_hbm, ids, sem, step, half).wait()
         if g + 1 < GROUP:
             widen(g + 1)
-        for u in range(g * PTS, (g + 1) * PTS):
-            i = idx_ref[0, 0, u]
-            tab = tabs[u % TABLES]
-            tab[pl.ds(i, 1), :] = tab[pl.ds(i, 1), :] + pay_ref[u : u + 1, :]
-
-
-def first_kernel(steps, idx_ref, in_ref, out_ref, pay_ref, *tabs):
+        for u in range(PTS):
+            i = ids[half][0, place * PTS + u]
+            tab = tabs[(g * PTS + u) % TABLES]
+            tab[pl.ds(i, 1), :] = tab[pl.ds(i, 1), :] + pay_ref[g * PTS + u : g * PTS + u + 1, :]
+        if place == GROUP // 2 - 1:
+            fetch(idx_hbm, ids, sem, later, half).start()
+
+
+def finish_fetch(steps, idx_hbm, ids, sem):
+    for half in range(2):
+        fetch(idx_hbm, ids, sem, steps - 1, half).wait()
+
+
+def first_kernel(steps, idx_hbm, in_ref, out_ref, pay_ref, ids0, ids1, sem, *tabs):
     step = pl.program_id(0)
     part = out_ref.shape[0]
+    ids = (ids0, ids1)
 
     @pl.when(step == 0)
     def _():
+        for half in range(2):
+            fetch(idx_hbm, ids, sem, 0, half).start()
         for tab in tabs:
             tab[...] = jnp.zeros_like(tab)
 
     @pl.when(step < steps)
     def _():
-        accumulate(idx_ref, in_ref, pay_ref, tabs)
+        accumulate(step, steps, idx_hbm, in_ref, pay_ref, ids, sem, tabs)
+
+    @pl.when(step == steps)
+    def _():
+        finish_fetch(steps, idx_hbm, ids, sem)
 
     @pl.when(step >= steps)
     def _():
@@ -198,22 +220,31 @@
         out_ref[...] = total
 
 
-def last_kernel(steps, idx_ref, in_ref, start_ref, out_ref, pay_ref, spread_ref, wide_ref, *tabs):
+def last_kernel(steps, idx_hbm, in_ref, start_hbm, out_ref, pay_ref, ids0, ids1, sem, spread_ref, wide_ref, got, *tabs):
     step = pl.program_id(0)
+    ids = (ids0, ids1)
 
     @pl.when(step == 0)
     def _():
-        for tab in tabs:
+        for half in range(2):
+            fetch(idx_hbm, ids, sem, 0, half).start()
+        pltpu.make_async_copy(start_hbm, tabs[0], got).start()
+        for tab in tabs[1:]:
             tab[...] = jnp.zeros_like(tab)
         source = lax.broadcasted_iota(jnp.int32, (CAMS, WIDTH), 0) * 9
         lane = lax.broadcasted_iota(jnp.int32, (CAMS, WIDTH), 1)
         spread = jnp.where((lane >= source) & (lane < source + 9), 1.0, 0.0).astype(jnp.bfloat16)
         spread_ref[0:CAMS, :] = spread
         spread_ref[CAMS : 2 * CAMS, :] = spread
+        pltpu.make_async_copy(start_hbm, tabs[0], got).wait()
 
     @pl.when(step < steps)
     def _():
-        accumulate(idx_ref, in_ref, pay_ref, tabs)
+        accumulate(step, steps, idx_hbm, in_ref, pay_ref, ids, sem, tabs)
+
+    @pl.when(step == steps)
+    def _():
+        finish_fetch(steps, idx_hbm, ids, sem)
 
     @pl.when(step >= steps)
     def _():
@@ -221,8 +252,8 @@
         parts = []
         for c in range(FINAL):
             rows = pl.ds(base + c * CAMS, CAMS)
-            total = start_ref[rows, :]
-            for tab in tabs:
+            total = tabs[0][rows, :]
+            for tab in tabs[1:]:
                 total = total + tab[rows, :]
             total = total.T[0:FEATS]
             high = total.astype(jnp.bfloat16)
@@ -249,25 +280,30 @@
 
 def index_of(arrived):
     cell = arrived[:, 36, :] * CAMS + arrived[:, 37, :]
-    return cell.astype(jnp.int32).reshape(SIDES // GROUP, 1, GROUP * PTS)
+    return cell.astype(jnp.int32).reshape(2 * SIDES // GROUP, 1, GROUP // 2 * PTS)
 
 
 def schur(in0, in1):
     steps = SIDES // GROUP
     cells = CAMS * CAMS
     part = 4096
-    spec_idx = pl.BlockSpec((1, 1, GROUP * PTS), lambda s: (jnp.minimum(s, steps - 1), 0, 0), memory_space=pltpu.SMEM)
     spec_in = pl.BlockSpec((GROUP, BLK, PTS), lambda s: (jnp.minimum(s, steps - 1), 0, 0))
     tabs = [pltpu.VMEM((cells, PTS), jnp.float32)] * TABLES
-    pay = pltpu.VMEM((GROUP * PTS, PTS), jnp.float32)
+    own = [
+        pltpu.VMEM((GROUP * PTS, PTS), jnp.float32),
+        pltpu.SMEM((1, GROUP // 2 * PTS), jnp.int32),
+        pltpu.SMEM((1, GROUP // 2 * PTS), jnp.int32),
+        pltpu.SemaphoreType.DMA((2,)),
+    ]
+    hbm = pl.BlockSpec(memory_space=pl.ANY)
     cost = pl.CostEstimate(flops=6 * 10**9, bytes_accessed=12 * 10**6, transcendentals=0)
     total = pl.pallas_call(
         functools.partial(first_kernel, steps),
         grid=(steps + cells // part,),
-        in_specs=[spec_idx, spec_in],
+        in_specs=[hbm, spec_in],
         out_specs=pl.BlockSpec((part, PTS), lambda s: (jnp.maximum(s - steps, 0), 0)),
         out_shape=jax.ShapeDtypeStruct((cells, PTS), jnp.float32),
-        scratch_shapes=[pay] + tabs,
+        scratch_shapes=own + tabs,
         compiler_params=params(),
         cost_estimate=cost,
         name="first",
@@ -275,13 +311,14 @@
     return pl.pallas_call(
         functools.partial(last_kernel, steps),
         grid=(steps + CAMS // FINAL,),
-        in_specs=[spec_idx, spec_in, pl.BlockSpec(memory_space=pltpu.VMEM)],
+        in_specs=[hbm, spec_in, hbm],
         out_specs=pl.BlockSpec((1, 9 * FINAL, WIDTH), lambda s: (0, jnp.maximum(s - steps, 0), 0)),
         out_shape=jax.ShapeDtypeStruct((1, WIDTH, WIDTH), jnp.float32),
-        scratch_shapes=[
-            pay,
+        scratch_shapes=own
+        + [
             pltpu.VMEM((2 * CAMS, WIDTH), jnp.bfloat16),
             pltpu.VMEM((FINAL * FEATS, WIDTH), jnp.float32),
+            pltpu.SemaphoreType.DMA(()),
         ]
         + tabs,
         compiler_params=params(),

time: 138 us -> 134 us (0.971)
  Pallas kernels: 87 us -> 77.9 us
  waiting for transfers between devices: 24.4 us -> 26.8 us
    pallas_call x1, Pallas kernels: 40 us -> 33.6 us  [schur(): pl.pallas_call(functools.partial(last_kernel, steps), grid=(steps + CAMS...]
    pallas_call x1, Pallas kernels: 28.5 us -> 25.8 us  [schur(): pl.pallas_call(functools.partial(first_kernel, steps), grid=(steps + cell...]
    all_to_all x1, waiting for transfers between devices: 5.67 us -> 8.06 us  [local(): lax.all_to_all(pack(1, shares.reshape(SIDES, 2, PTS)), RC, 0, 0, tiled=True)]
  transfers between devices with their start and end apart: 3 -> 3, of which waited for: 3 -> 3; matrix products, arithmetic and copies ran while one was open for 4% -> 4% of each run, Pallas kernels for 30% -> 29%
where the time goes in v4:
time: 134 us
  Pallas kernels  77.9 us (58%)
  waiting for transfers between devices  26.8 us (20%)
  starting transfers between devices  18.6 us (14%)
  other arithmetic  5.06 us (4%)
  local copies, waits for them, and re-layouts  4.47 us (3%)
    pallas_call x1, Pallas kernels, schur(): pl.pallas_call(functools.partial(last_kernel, steps), grid=(steps + CAMS...  33.6 us
    pallas_call x1, Pallas kernels, schur(): pl.pallas_call(functools.partial(first_kernel, steps), grid=(steps + cell...  25.8 us
    all_to_all x1, waiting for transfers between devices, local(): in0 = lax.all_to_all(pack(0), RC, 0, 0, tiled=True)  17.7 us
    all_to_all x1, starting transfers between devices, local(): in0 = lax.all_to_all(pack(0), RC, 0, 0, tiled=True)  11.9 us
    pallas_call x2, Pallas kernels, pack(): pl.pallas_call(functools.partial(pack_kernel, which), in_specs=[smem] * 3...  11.4 us
    all_to_all x1, waiting for transfers between devices, local(): lax.all_to_all(pack(1, shares.reshape(SIDES, 2, PTS)), RC, 0, 0, tiled=True)  8.06 us
    pallas_call x1, Pallas kernels, local(): pl.pallas_call(rhs_kernel, in_specs=[smem] * 3 + [vmem] * 5, out_specs=vm...  7.11 us
    all_to_all x1, starting transfers between devices, local(): lax.all_to_all(pack(1, shares.reshape(SIDES, 2, PTS)), RC, 0, 0, tiled=True)  5.5 us
  transfers between devices with their start and end apart: 3, of which 3 were waited for; matrix products, arithmetic and copies ran while one was open for 4% of the time, Pallas kernels for 29%

profile of v4, /device:TPU:1, one launch (start us, length us, event | category | flops | bytes accessed | tf_op | source)
XLA Modules:
  0.0 133.7 jit_solution(1665822605109014209)
XLA Ops:
  0.6 6.1 %pack0.1 = f32[128,40,128]{2,1,0:T(8,128)} custom-call(s32[64]{0:T(128)} %bitcast.32, s32[2,64]{1,0:T(2,128)} %bitcast.29, s32[32]{0:T(128)} %refs_2_.3, f32[36,64,128]{2,1,0:T(8,128)} %bitcast.17, f32[12,64,128]{2,1,0:T(8,128)} %bitcast.21, f32[64,128]{1,0:T(8,128)} %refs_5_.3, s32[64,2,128]{2,1,0:T(2,128)} %refs_6_.3), custom_call_target="tpu_custom_call" | custom-call | flops 10000000 | bytes 6000000 | tf_op jit(solution)/shard_map/pack0/pallas_call | solution.py:339
  6.8 11.9 %all-to-all-start.1 = ((f32[128,40,128]{2,1,0:T(8,128)}), f32[128,40,128]{2,1,0:T(8,128)}, u32[]{:S(2)}, u32[]{:S(2)}) async-start(f32[128,40,128]{2,1,0:T(8,128)} %pack0.1), calls=%async_computation.1 | async-start | bytes 5242880 | tf_op jit(solution)/shard_map/all_to_all | solution.py:354
  18.7 7.1 %rhs.1 = f32[32,16,128]{2,1,0:T(8,128)} custom-call(s32[64]{0:T(128)} %bitcast.33, s32[2,64]{1,0:T(2,128)} %bitcast.30, s32[32]{0:T(128)} %refs_2_.3, f32[36,64,128]{2,1,0:T(8,128)} %bitcast.18, f32[12,64,128]{2,1,0:T(8,128)} %bitcast.22, f32[64,4,128]{2,1,0:T(4,128)} %res_ref.1, f32[64,128]{1,0:T(8,128)} %refs_5_.3, s32[64,2,128]{2,1,0:T(2,128)} %refs_6_.3), custom_call_target="tpu_custom_call" | custom-call | flops 10000000000 | bytes 3000000 | tf_op jit(solution)/shard_map/rhs/pallas_call | solution.py:356
  25.8 0.9 dynamic-slice_bitcast_fusion
  26.7 1.2 collective-permute-start
  27.9 1.0 collective-permute-done
  28.9 0.9 bitcast_add_fusion
  29.8 0.3 reshape.83
  30.2 0.2 copy.12
  30.3 1.1 reshape.84.refs_7_
  31.5 5.3 %pack1.1 = f32[128,40,128]{2,1,0:T(8,128)} custom-call(s32[64]{0:T(128)} %bitcast.34, s32[2,64]{1,0:T(2,128)} %bitcast.31, s32[32]{0:T(128)} %refs_2_.3, f32[36,64,128]{2,1,0:T(8,128)} %bitcast.19, f32[12,64,128]{2,1,0:T(8,128)} %bitcast.23, f32[64,128]{1,0:T(8,128)} %refs_5_.3, s32[64,2,128]{2,1,0:T(2,128)} %refs_6_.3, f32[128,2,128]{2,1,0:T(2,128)} %reshape.84.refs_7_), custom_call_target="tpu_custom_call" | custom-call | flops 10000000 | bytes 6000000 | tf_op jit(solution)/shard_map/pack1/pallas_call | solution.py:339
  36.8 17.7 %all-to-all-done.1.in_ref = f32[128,40,128]{2,1,0:T(8,128)} async-done(((f32[128,40,128]{2,1,0:T(8,128)}), f32[128,40,128]{2,1,0:T(8,128)}, u32[]{:S(2)}, u32[]{:S(2)}) %all-to-all-start.1) | async-done | bytes 2621472 | tf_op jit(solution)/shard_map/all_to_all | solution.py:354
  54.5 5.5 %all-to-all-start = ((f32[128,40,128]{2,1,0:T(8,128)}), f32[128,40,128]{2,1,0:T(8,128)}, u32[]{:S(2)}, u32[]{:S(2)}) async-start(f32[128,40,128]{2,1,0:T(8,128)} %pack1.1), calls=%async_computation | async-start | bytes 5242880 | tf_op jit(solution)/shard_map/all_to_all | solution.py:372
  60.0 2.0 %fusion = s32[128,1,128]{2,1,0:T(1,128)} fusion(f32[128,40,128]{2,1,0:T(8,128)} %all-to-all-done.1.in_ref), kind=kLoop, calls=%fused_computation.3 | loop fusion | flops 49152 | bytes 196608 | tf_op jit(solution)/shard_map/convert_element_type | solution.py:283
  62.0 25.8 %first.1.start_hbm = f32[16384,128]{1,0:T(8,128)} custom-call(s32[16,1,1024]{2,1,0:T(1,128)} %bitcast.28, f32[128,40,128]{2,1,0:T(8,128)} %all-to-all-done.1.in_ref), custom_call_target="tpu_custom_call" | custom-call | flops 6000000000 | bytes 12000000 | tf_op jit(solution)/shard_map/first/pallas_call | solution.py:300
  87.9 8.1 %all-to-all-done.in_ref = f32[128,40,128]{2,1,0:T(8,128)} async-done(((f32[128,40,128]{2,1,0:T(8,128)}), f32[128,40,128]{2,1,0:T(8,128)}, u32[]{:S(2)}, u32[]{:S(2)}) %all-to-all-start) | async-done | bytes 2621472 | tf_op jit(solution)/shard_map/all_to_all | solution.py:372
  95.9 1.1 slice.28
  97.0 0.1 reduce_sum.9
  97.1 0.1 reshape.86
  97.2 0.1 copy.15
  97.3 0.7 reshape.87
  98.0 2.0 %fusion.1 = s32[128,1,128]{2,1,0:T(1,128)} fusion(f32[128,40,128]{2,1,0:T(8,128)} %all-to-all-done.in_ref), kind=kLoop, calls=%fused_computation.6 | loop fusion | flops 49152 | bytes 196608 | tf_op jit(solution)/shard_map/convert_element_type | solution.py:283
  100.0 33.6 %last.1 = f32[1,1152,1152]{2,1,0:T(8,128)} custom-call(s32[16,1,1024]{2,1,0:T(1,128)} %bitcast.27, f32[128,40,128]{2,1,0:T(8,128)} %all-to-all-done.in_ref, f32[16384,128]{1,0:T(8,128)} %first.1.start_hbm), custom_call_target="tpu_custom_call" | custom-call | flops 6000000000 | bytes 12000000 | tf_op jit(solution)/shard_map/last/pallas_call | solution.py:311
  (1 shorter events, 0.0 us)
Async XLA Ops:
  6.8 47.7 %all-to-all-start.1 = ((f32[128,40,128]{2,1,0:T(8,128)}), f32[128,40,128]{2,1,0:T(8,128)}, u32[]{:S(2)}, u32[]{:S(2)}) async-start(f32[128,40,128]{2,1,0:T(8,128)} %pack0.1), calls=%async_computation.1 | async-start | bytes 5242880 | tf_op jit(solution)/shard_map/all_to_all | solution.py:354
  26.7 2.2 %collective-permute-start = (f32[16,16,128]{2,1,0:T(8,128)S(1)}, f32[16,16,128]{2,1,0:T(8,128)S(1)}, u32[]{:S(2)}, u32[]{:S(2)}) collective-permute-start(f32[16,16,128]{2,1,0:T(8,128)S(1)} %dynamic-slice_bitcast_fusion), channel_id=1, source_target_pairs={{0,1},{1,0},{2,3},{3,2},{4,5},{5,4},{6,7},{7,6},{8,9},{9,8},{10,11... | collective-permute-start | bytes 393224 | tf_op jit(solution)/shard_map/ppermute | solution.py:370
  54.5 41.4 %all-to-all-start = ((f32[128,40,128]{2,1,0:T(8,128)}), f32[128,40,128]{2,1,0:T(8,128)}, u32[]{:S(2)}, u32[]{:S(2)}) async-start(f32[128,40,128]{2,1,0:T(8,128)} %pack1.1), calls=%async_computation | async-start | bytes 5242880 | tf_op jit(solution)/shard_map/all_to_all | solution.py:372

commit v5 on v4

--- a/solution.py
+++ b/solution.py
@@ -14,9 +14,11 @@
 SIDES = 128
 CLUSTERS = 32
 BLK = 40
-GROUP = 16
-TABLES = 6
-FINAL = 16
+GROUP = 32
+TABLES = 2
+RUN = 8
+FLAG = 1 << 16
+FINAL = 32
 FEATS = 88
 VMEM_LIMIT = 62 * 2**20
 RC = ("row", "col")
@@ -93,6 +95,24 @@
         turn(6 + o, zero)
     tops = 38 if which else BLK
 
+    def write(t):
+        pair = bp_ref[t]
+        first, second = slot_of(ps_ref[0, pair], home_ref), slot_of(ps_ref[1, pair], home_ref)
+        base = pl.multiple_of(t * BLK, 8)
+        out_ref[first, 0:tops, :] = rows_ref[pl.ds(base, tops), :]
+        out_ref[second, 0:16, :] = rows_ref[pl.ds(base + 16, 16), :]
+        out_ref[second, 16:32, :] = rows_ref[pl.ds(base, 16), :]
+        out_ref[second, 32:tops, :] = turned_ref[pl.ds(pl.multiple_of(t * 8, 8), tops - 32), :]
+
+    if which == 0:
+
+        def back(n, carry):
+            write(blocks - 1 - n)
+            return carry
+
+        lax.fori_loop(0, blocks, back, 0, unroll=4)
+        return
+
     def clear(i, carry):
         seen_ref[i] = 0
         return carry
@@ -103,16 +123,7 @@
         pair = bp_ref[t]
         rank = seen_ref[pair]
         seen_ref[pair] = rank + 1
-
-        @pl.when(rank == which)
-        def _():
-            first, second = slot_of(ps_ref[0, pair], home_ref), slot_of(ps_ref[1, pair], home_ref)
-            base = pl.multiple_of(t * BLK, 8)
-            out_ref[first, 0:tops, :] = rows_ref[pl.ds(base, tops), :]
-            out_ref[second, 0:16, :] = rows_ref[pl.ds(base + 16, 16), :]
-            out_ref[second, 16:32, :] = rows_ref[pl.ds(base, 16), :]
-            out_ref[second, 32:tops, :] = turned_ref[pl.ds(pl.multiple_of(t * 8, 8), tops - 32), :]
-
+        pl.when(rank == which)(lambda: write(t))
         return carry
 
     lax.fori_loop(0, blocks, one, 0)
@@ -160,11 +171,23 @@
     return rows
 
 
-def fetch(idx_hbm, ids, sem, step, half):
-    return pltpu.make_async_copy(idx_hbm.at[2 * step + half], ids[half], sem.at[half])
-
-
-def accumulate(step, steps, idx_hbm, in_ref, pay_ref, ids, sem, tabs):
+def fetch(cells_ref, ids, sem, step, half):
+    rows = pl.ds(pl.multiple_of((2 * step + half) * (GROUP // 2), GROUP // 2), GROUP // 2)
+    return pltpu.make_async_copy(cells_ref.at[rows, :], ids[half], sem.at[half])
+
+
+def name_cells(tail_ref, cells_ref):
+    cell = tail_ref[:, 4, :] * CAMS + tail_ref[:, 5, :]
+    lane = lax.broadcasted_iota(jnp.int32, (SIDES, PTS), 1)
+    hits = jnp.zeros((SIDES, PTS), jnp.float32)
+    for r in range(1, RUN):
+        same = (cell == pltpu.roll(cell, r, 1)) & (lane % RUN >= r)
+        hits = jnp.where(same, 1.0, hits)
+    flag = jnp.max(hits, axis=1, keepdims=True) * float(FLAG)
+    cells_ref[...] = jnp.where(lane == 0, cell + flag, cell).astype(jnp.int32)
+
+
+def accumulate(step, steps, in_ref, pay_ref, cells_ref, ids, sem, tabs):
     def widen(g):
         rows = expand(in_ref[g])
         rows.append(jnp.zeros((CAMS - FEATS, PTS), jnp.float32))
@@ -174,42 +197,72 @@
     widen(0)
     for g in range(GROUP):
         half, place = divmod(g, GROUP // 2)
+        mine = ids[half]
         if place == 0:
-            fetch(idx_hbm, ids, sem, step, half).wait()
-        if g + 1 < GROUP:
-            widen(g + 1)
-        for u in range(PTS):
-            i = ids[half][0, place * PTS + u]
-            tab = tabs[(g * PTS + u) % TABLES]
-            tab[pl.ds(i, 1), :] = tab[pl.ds(i, 1), :] + pay_ref[g * PTS + u : g * PTS + u + 1, :]
+            fetch(cells_ref, ids, sem, step, half).wait()
+        start = mine[place, 0]
+
+        @pl.when(start < FLAG)
+        def _():
+            if g + 1 < GROUP:
+                widen(g + 1)
+            for k in range(PTS // RUN):
+                tab = tabs[k % TABLES]
+                here = range(k * RUN, (k + 1) * RUN)
+                at = [mine[place, u] for u in here]
+                old = [tab[pl.ds(i, 1), :] for i in at]
+                for u, i, value in zip(here, at, old):
+                    tab[pl.ds(i, 1), :] = value + pay_ref[g * PTS + u : g * PTS + u + 1, :]
+
+        @pl.when(start >= FLAG)
+        def _():
+            if g + 1 < GROUP:
+                widen(g + 1)
+
+            def single(u, carry):
+                i = mine[place, u]
+                i = jnp.where(i >= FLAG, i - FLAG, i)
+                tabs[0][pl.ds(i, 1), :] = tabs[0][pl.ds(i, 1), :] + pay_ref[pl.ds(g * PTS + u, 1), :]
+                return carry
+
+            lax.fori_loop(0, PTS, single, 0, unroll=8)
+
         if place == GROUP // 2 - 1:
-            fetch(idx_hbm, ids, sem, later, half).start()
-
-
-def finish_fetch(steps, idx_hbm, ids, sem):
+            fetch(cells_ref, ids, sem, later, half).start()
+
+
+def finish_fetch(steps, cells_ref, ids, sem):
     for half in range(2):
-        fetch(idx_hbm, ids, sem, steps - 1, half).wait()
-
-
-def first_kernel(steps, idx_hbm, in_ref, out_ref, pay_ref, ids0, ids1, sem, *tabs):
+        fetch(cells_ref, ids, sem, steps - 1, half).wait()
+
+
+def begin(in_hbm, tail_ref, cells_ref, ids, sem, tail_sem, tabs):
+    tail = pltpu.make_async_copy(in_hbm.at[:, 32:40, :], tail_ref, tail_sem)
+    tail.start()
+    for tab in tabs:
+        tab[...] = jnp.zeros_like(tab)
+    tail.wait()
+    name_cells(tail_ref, cells_ref)
+    for half in range(2):
+        fetch(cells_ref, ids, sem, 0, half).start()
+
+
+def first_kernel(steps, in_hbm, in_ref, out_ref, pay_ref, tail_ref, cells_ref, ids0, ids1, sem, tail_sem, *tabs):
     step = pl.program_id(0)
     part = out_ref.shape[0]
     ids = (ids0, ids1)
 
     @pl.when(step == 0)
     def _():
-        for half in range(2):
-            fetch(idx_hbm, ids, sem, 0, half).start()
-        for tab in tabs:
-            tab[...] = jnp.zeros_like(tab)
+        begin(in_hbm, tail_ref, cells_ref, ids, sem, tail_sem, tabs)
 
     @pl.when(step < steps)
     def _():
-        accumulate(step, steps, idx_hbm, in_ref, pay_ref, ids, sem, tabs)
+        accumulate(step, steps, in_ref, pay_ref, cells_ref, ids, sem, tabs)
 
     @pl.when(step == steps)
     def _():
-        finish_fetch(steps, idx_hbm, ids, sem)
+        finish_fetch(steps, cells_ref, ids, sem)
 
     @pl.when(step >= steps)
     def _():
@@ -220,31 +273,45 @@
         out_ref[...] = total
 
 
-def last_kernel(steps, idx_hbm, in_ref, start_hbm, out_ref, pay_ref, ids0, ids1, sem, spread_ref, wide_ref, got, *tabs):
+def collect_rhs(tail_ref, rhs_ref):
+    share = rhs_ref.shape[1]
+    sums = jnp.sum(tail_ref[...].reshape(SIDES // 2, 2, 8, PTS), axis=0).reshape(16, PTS)
+    lane = lax.broadcasted_iota(jnp.int32, (PTS, share), 0)
+    place = lax.broadcasted_iota(jnp.int32, (PTS, share), 1)
+    eight = jnp.where(place == 9 * (lane % 16) + lane // 16, 1.0, 0.0)
+    last = jnp.where((place == 9 * lane + 8) & (lane < 16), 1.0, 0.0)
+    exact = lax.Precision.HIGHEST
+    upper = jnp.dot(sums, eight, precision=exact, preferred_element_type=jnp.float32)
+    lower = jnp.dot(sums, last, precision=exact, preferred_element_type=jnp.float32)
+    rhs_ref[0:1, :] = upper[6:7] + lower[7:8]
+    rhs_ref[1:2, :] = upper[14:15] + lower[15:16]
+
+
+def last_kernel(steps, in_hbm, in_ref, start_hbm, out_ref, rhs_ref, pay_ref, tail_ref, cells_ref, ids0, ids1, sem, tail_sem, *refs):
+    spread_ref, wide_ref, start_ref, got = refs[:4]
+    tabs = refs[4:]
     step = pl.program_id(0)
     ids = (ids0, ids1)
 
     @pl.when(step == 0)
     def _():
-        for half in range(2):
-            fetch(idx_hbm, ids, sem, 0, half).start()
-        pltpu.make_async_copy(start_hbm, tabs[0], got).start()
-        for tab in tabs[1:]:
-            tab[...] = jnp.zeros_like(tab)
+        pltpu.make_async_copy(start_hbm, start_ref, got).start()
+        begin(in_hbm, tail_ref, cells_ref, ids, sem, tail_sem, tabs)
+        collect_rhs(tail_ref, rhs_ref)
         source = lax.broadcasted_iota(jnp.int32, (CAMS, WIDTH), 0) * 9
         lane = lax.broadcasted_iota(jnp.int32, (CAMS, WIDTH), 1)
         spread = jnp.where((lane >= source) & (lane < source + 9), 1.0, 0.0).astype(jnp.bfloat16)
         spread_ref[0:CAMS, :] = spread
         spread_ref[CAMS : 2 * CAMS, :] = spread
-        pltpu.make_async_copy(start_hbm, tabs[0], got).wait()
 
     @pl.when(step < steps)
     def _():
-        accumulate(step, steps, idx_hbm, in_ref, pay_ref, ids, sem, tabs)
+        accumulate(step, steps, in_ref, pay_ref, cells_ref, ids, sem, tabs)
 
     @pl.when(step == steps)
     def _():
-        finish_fetch(steps, idx_hbm, ids, sem)
+        finish_fetch(steps, cells_ref, ids, sem)
+        pltpu.make_async_copy(start_hbm, start_ref, got).wait()
 
     @pl.when(step >= steps)
     def _():
@@ -252,8 +319,8 @@
         parts = []
         for c in range(FINAL):
             rows = pl.ds(base + c * CAMS, CAMS)
-            total = tabs[0][rows, :]
-            for tab in tabs[1:]:
+            total = start_ref[rows, :]
+            for tab in tabs:
                 total = total + tab[rows, :]
             total = total.T[0:FEATS]
             high = total.astype(jnp.bfloat16)
@@ -278,22 +345,21 @@
     return pltpu.CompilerParams(vmem_limit_bytes=VMEM_LIMIT, **more)
 
 
-def index_of(arrived):
-    cell = arrived[:, 36, :] * CAMS + arrived[:, 37, :]
-    return cell.astype(jnp.int32).reshape(2 * SIDES // GROUP, 1, GROUP // 2 * PTS)
-
-
 def schur(in0, in1):
     steps = SIDES // GROUP
     cells = CAMS * CAMS
-    part = 4096
+    part = 8192
     spec_in = pl.BlockSpec((GROUP, BLK, PTS), lambda s: (jnp.minimum(s, steps - 1), 0, 0))
     tabs = [pltpu.VMEM((cells, PTS), jnp.float32)] * TABLES
+    half = pltpu.SMEM((GROUP // 2, PTS), jnp.int32)
     own = [
         pltpu.VMEM((GROUP * PTS, PTS), jnp.float32),
-        pltpu.SMEM((1, GROUP // 2 * PTS), jnp.int32),
-        pltpu.SMEM((1, GROUP // 2 * PTS), jnp.int32),
+        pltpu.VMEM((SIDES, 8, PTS), jnp.float32),
+        pltpu.VMEM((SIDES, PTS), jnp.int32),
+        half,
+        half,
         pltpu.SemaphoreType.DMA((2,)),
+        pltpu.SemaphoreType.DMA(()),
     ]
     hbm = pl.BlockSpec(memory_space=pl.ANY)
     cost = pl.CostEstimate(flops=6 * 10**9, bytes_accessed=12 * 10**6, transcendentals=0)
@@ -307,24 +373,31 @@
         compiler_params=params(),
         cost_estimate=cost,
         name="first",
-    )(index_of(in0), in0)
+    )(in0, in0)
     return pl.pallas_call(
         functools.partial(last_kernel, steps),
         grid=(steps + CAMS // FINAL,),
         in_specs=[hbm, spec_in, hbm],
-        out_specs=pl.BlockSpec((1, 9 * FINAL, WIDTH), lambda s: (0, jnp.maximum(s - steps, 0), 0)),
-        out_shape=jax.ShapeDtypeStruct((1, WIDTH, WIDTH), jnp.float32),
+        out_specs=[
+            pl.BlockSpec((1, 9 * FINAL, WIDTH), lambda s: (0, jnp.maximum(s - steps, 0), 0)),
+            pl.BlockSpec((2, WIDTH // 8), lambda s: (0, 0)),
+        ],
+        out_shape=[
+            jax.ShapeDtypeStruct((1, WIDTH, WIDTH), jnp.float32),
+            jax.ShapeDtypeStruct((2, WIDTH // 8), jnp.float32),
+        ],
         scratch_shapes=own
         + [
             pltpu.VMEM((2 * CAMS, WIDTH), jnp.bfloat16),
             pltpu.VMEM((FINAL * FEATS, WIDTH), jnp.float32),
+            pltpu.VMEM((cells, PTS), jnp.float32),
             pltpu.SemaphoreType.DMA(()),
         ]
         + tabs,
         compiler_params=params(),
         cost_estimate=cost,
         name="last",
-    )(index_of(in1), in1, total)
+    )(in1, in1, total)
 
 
 def local(cam_jac, pt_jac, resid, damping, cams, block_pair, pair_sides, cluster_home):
@@ -370,10 +443,7 @@
     mine = mine + lax.ppermute(other, "col", [(c, c ^ 1) for c in range(cols)])
     shares = jnp.transpose(mine.reshape(rows, 16, cols, CAMS // cols), (0, 2, 1, 3))
     in1 = lax.all_to_all(pack(1, shares.reshape(SIDES, 2, PTS)), RC, 0, 0, tiled=True)
-    share = jnp.sum(in1[:, 38:40, :].reshape(SIDES // 2, 2, 2, PTS), axis=0).reshape(2, 16, CAMS // cols)
-    reduced_rhs = jnp.transpose(share[:, 0:9], (0, 2, 1)).reshape(2, WIDTH // cols)
-
-    return schur(in0, in1), reduced_rhs
+    return schur(in0, in1)
 
 
 def solution(mesh):

time: 134 us -> 126 us (0.940)
  Pallas kernels: 77.9 us -> 69.5 us
  waiting for transfers between devices: 26.8 us -> 32.1 us
  other arithmetic: 5.06 us -> 0.92 us
  local copies, waits for them, and re-layouts: 4.47 us -> 2.52 us
    all_to_all x1, waiting for transfers between devices: 8.06 us -> 13.5 us  [local(): lax.all_to_all(pack(1, shares.reshape(SIDES, 2, PTS)), RC, 0, 0, tiled=True)]
    convert_element_type x2 -> x0, other arithmetic: 4.04 us -> none  [index_of(): cell.astype(jnp.int32).reshape(2 * SIDES // GROUP, 1, GROUP // 2 * PTS)]
    pallas_call x1, Pallas kernels: 33.6 us -> 29.9 us  [schur(): pl.pallas_call(functools.partial(last_kernel, steps), grid=(steps + CAMS...]
    pallas_call x1, Pallas kernels: 25.8 us -> 22.4 us  [schur(): pl.pallas_call(functools.partial(first_kernel, steps), grid=(steps + cell...]
  transfers between devices with their start and end apart: 3 -> 3, of which waited for: 3 -> 3; matrix products, arithmetic and copies ran while one was open for 4% -> 3% of each run, Pallas kernels for 29% -> 28%
where the time goes in v5:
time: 126 us; the launch traced here: 125 us
  Pallas kernels  69.5 us (55%)
  waiting for transfers between devices  32.1 us (25%)
  starting transfers between devices  18.6 us (15%)
  local copies, waits for them, and re-layouts  2.52 us (2%)
    pallas_call x1, Pallas kernels, schur(): pl.pallas_call(functools.partial(last_kernel, steps), grid=(steps + CAMS...  29.9 us
    pallas_call x1, Pallas kernels, schur(): pl.pallas_call(functools.partial(first_kernel, steps), grid=(steps + cell...  22.4 us
    all_to_all x1, waiting for transfers between devices, local(): in0 = lax.all_to_all(pack(0), RC, 0, 0, tiled=True)  17.7 us
    all_to_all x1, waiting for transfers between devices, local(): lax.all_to_all(pack(1, shares.reshape(SIDES, 2, PTS)), RC, 0, 0, tiled=True)  13.5 us
    all_to_all x1, starting transfers between devices, local(): in0 = lax.all_to_all(pack(0), RC, 0, 0, tiled=True)  11.9 us
    pallas_call x2, Pallas kernels, pack(): pl.pallas_call(functools.partial(pack_kernel, which), in_specs=[smem] * 3...  10.1 us
    pallas_call x1, Pallas kernels, local(): pl.pallas_call(rhs_kernel, in_specs=[smem] * 3 + [vmem] * 5, out_specs=vm...  7.11 us
    all_to_all x1, starting transfers between devices, local(): lax.all_to_all(pack(1, shares.reshape(SIDES, 2, PTS)), RC, 0, 0, tiled=True)  5.52 us
  transfers between devices with their start and end apart: 3, of which 3 were waited for; matrix products, arithmetic and copies ran while one was open for 3% of the time, Pallas kernels for 28%

profile of v5, /device:TPU:1, one launch (start us, length us, event | category | flops | bytes accessed | tf_op | source)
XLA Modules:
  0.0 124.6 jit_solution(8997353540123158063)
XLA Ops:
  0.6 4.8 %pack0.1 = f32[128,40,128]{2,1,0:T(8,128)} custom-call(s32[64]{0:T(128)} %bitcast.24, s32[2,64]{1,0:T(2,128)} %bitcast.21, s32[32]{0:T(128)} %refs_2_.3, f32[36,64,128]{2,1,0:T(8,128)} %bitcast.12, f32[12,64,128]{2,1,0:T(8,128)} %bitcast.16, f32[64,128]{1,0:T(8,128)} %refs_5_.3, s32[64,2,128]{2,1,0:T(2,128)} %refs_6_.3), custom_call_target="tpu_custom_call" | custom-call | flops 10000000 | bytes 6000000 | tf_op jit(solution)/shard_map/pack0/pallas_call | solution.py:412
  5.4 11.9 %all-to-all-start.1 = ((f32[128,40,128]{2,1,0:T(8,128)}), f32[128,40,128]{2,1,0:T(8,128)}, u32[]{:S(2)}, u32[]{:S(2)}) async-start(f32[128,40,128]{2,1,0:T(8,128)} %pack0.1), calls=%async_computation.1 | async-start | bytes 5242880 | tf_op jit(solution)/shard_map/all_to_all | solution.py:427
  17.3 7.1 %rhs.1 = f32[32,16,128]{2,1,0:T(8,128)} custom-call(s32[64]{0:T(128)} %bitcast.25, s32[2,64]{1,0:T(2,128)} %bitcast.22, s32[32]{0:T(128)} %refs_2_.3, f32[36,64,128]{2,1,0:T(8,128)} %bitcast.13, f32[12,64,128]{2,1,0:T(8,128)} %bitcast.17, f32[64,4,128]{2,1,0:T(4,128)} %res_ref.1, f32[64,128]{1,0:T(8,128)} %refs_5_.3, s32[64,2,128]{2,1,0:T(2,128)} %refs_6_.3), custom_call_target="tpu_custom_call" | custom-call | flops 10000000000 | bytes 3000000 | tf_op jit(solution)/shard_map/rhs/pallas_call | solution.py:429
  24.4 0.9 dynamic-slice_bitcast_fusion
  25.4 1.2 collective-permute-start
  26.6 1.0 collective-permute-done
  27.6 0.9 bitcast_add_fusion
  28.5 0.3 reshape.18
  28.8 0.2 copy.10
  29.0 1.1 reshape.19.refs_7_
  30.1 5.3 %pack1.1 = f32[128,40,128]{2,1,0:T(8,128)} custom-call(s32[64]{0:T(128)} %bitcast.26, s32[2,64]{1,0:T(2,128)} %bitcast.23, s32[32]{0:T(128)} %refs_2_.3, f32[36,64,128]{2,1,0:T(8,128)} %bitcast.14, f32[12,64,128]{2,1,0:T(8,128)} %bitcast.18, f32[64,128]{1,0:T(8,128)} %refs_5_.3, s32[64,2,128]{2,1,0:T(2,128)} %refs_6_.3, f32[128,2,128]{2,1,0:T(2,128)} %reshape.19.refs_7_), custom_call_target="tpu_custom_call" | custom-call | flops 10000000 | bytes 6000000 | tf_op jit(solution)/shard_map/pack1/pallas_call | solution.py:412
  35.4 17.7 %all-to-all-done.1.in_hbm.in_ref = f32[128,40,128]{2,1,0:T(8,128)} async-done(((f32[128,40,128]{2,1,0:T(8,128)}), f32[128,40,128]{2,1,0:T(8,128)}, u32[]{:S(2)}, u32[]{:S(2)}) %all-to-all-start.1) | async-done | bytes 2621472 | tf_op jit(solution)/shard_map/all_to_all | solution.py:427
  53.1 5.5 %all-to-all-start = ((f32[128,40,128]{2,1,0:T(8,128)}), f32[128,40,128]{2,1,0:T(8,128)}, u32[]{:S(2)}, u32[]{:S(2)}) async-start(f32[128,40,128]{2,1,0:T(8,128)} %pack1.1), calls=%async_computation | async-start | bytes 5242880 | tf_op jit(solution)/shard_map/all_to_all | solution.py:445
  58.6 22.4 %first.1.start_hbm = f32[16384,128]{1,0:T(8,128)} custom-call(f32[128,40,128]{2,1,0:T(8,128)} %all-to-all-done.1.in_hbm.in_ref, f32[128,40,128]{2,1,0:T(8,128)} %all-to-all-done.1.in_hbm.in_ref), custom_call_target="tpu_custom_call" | custom-call | flops 6000000000 | bytes 12000000 | tf_op jit(solution)/shard_map/first/pallas_call | solution.py:366
  81.1 13.5 %all-to-all-done.in_hbm.in_ref = f32[128,40,128]{2,1,0:T(8,128)} async-done(((f32[128,40,128]{2,1,0:T(8,128)}), f32[128,40,128]{2,1,0:T(8,128)}, u32[]{:S(2)}, u32[]{:S(2)}) %all-to-all-start) | async-done | bytes 2621472 | tf_op jit(solution)/shard_map/all_to_all | solution.py:445
  94.6 29.9 %last.1 = (f32[1,1152,1152]{2,1,0:T(8,128)}, f32[2,144]{1,0:T(2,128)}) custom-call(f32[128,40,128]{2,1,0:T(8,128)} %all-to-all-done.in_hbm.in_ref, f32[128,40,128]{2,1,0:T(8,128)} %all-to-all-done.in_hbm.in_ref, f32[16384,128]{1,0:T(8,128)} %first.1.start_hbm), custom_call_target="tpu_custom_call" | custom-call | flops 6000000000 | bytes 12000000 | tf_op jit(solution)/shard_map/last/pallas_call | solution.py:377
Async XLA Ops:
  5.4 47.7 %all-to-all-start.1 = ((f32[128,40,128]{2,1,0:T(8,128)}), f32[128,40,128]{2,1,0:T(8,128)}, u32[]{:S(2)}, u32[]{:S(2)}) async-start(f32[128,40,128]{2,1,0:T(8,128)} %pack0.1), calls=%async_computation.1 | async-start | bytes 5242880 | tf_op jit(solution)/shard_map/all_to_all | solution.py:427
  25.4 2.2 %collective-permute-start = (f32[16,16,128]{2,1,0:T(8,128)S(1)}, f32[16,16,128]{2,1,0:T(8,128)S(1)}, u32[]{:S(2)}, u32[]{:S(2)}) collective-permute-start(f32[16,16,128]{2,1,0:T(8,128)S(1)} %dynamic-slice_bitcast_fusion), channel_id=1, source_target_pairs={{0,1},{1,0},{2,3},{3,2},{4,5},{5,4},{6,7},{7,6},{8,9},{9,8},{10,11... | collective-permute-start | bytes 393224 | tf_op jit(solution)/shard_map/ppermute | solution.py:443
  53.1 41.5 %all-to-all-start = ((f32[128,40,128]{2,1,0:T(8,128)}), f32[128,40,128]{2,1,0:T(8,128)}, u32[]{:S(2)}, u32[]{:S(2)}) async-start(f32[128,40,128]{2,1,0:T(8,128)} %pack1.1), calls=%async_computation | async-start | bytes 5242880 | tf_op jit(solution)/shard_map/all_to_all | solution.py:445

commit v6 on v5

--- a/solution.py
+++ b/solution.py
@@ -19,6 +19,7 @@
 RUN = 8
 FLAG = 1 << 16
 FINAL = 32
+PART = 16
 FEATS = 88
 VMEM_LIMIT = 62 * 2**20
 RC = ("row", "col")
@@ -219,13 +220,16 @@
             if g + 1 < GROUP:
                 widen(g + 1)
 
-            def single(u, carry):
-                i = mine[place, u]
-                i = jnp.where(i >= FLAG, i - FLAG, i)
-                tabs[0][pl.ds(i, 1), :] = tabs[0][pl.ds(i, 1), :] + pay_ref[pl.ds(g * PTS + u, 1), :]
+            def several(n, carry):
+                for v in range(8):
+                    u = n * 8 + v
+                    tab = tabs[v % TABLES]
+                    i = mine[place, u]
+                    i = jnp.where(i >= FLAG, i - FLAG, i)
+                    tab[pl.ds(i, 1), :] = tab[pl.ds(i, 1), :] + pay_ref[pl.ds(g * PTS + u, 1), :]
                 return carry
 
-            lax.fori_loop(0, PTS, single, 0, unroll=8)
+            lax.fori_loop(0, PTS // 8, several, 0)
 
         if place == GROUP // 2 - 1:
             fetch(cells_ref, ids, sem, later, half).start()
@@ -316,29 +320,46 @@
     @pl.when(step >= steps)
     def _():
         base = pl.multiple_of((step - steps) * FINAL * CAMS, FINAL * CAMS)
-        parts = []
-        for c in range(FINAL):
-            rows = pl.ds(base + c * CAMS, CAMS)
-            total = start_ref[rows, :]
-            for tab in tabs:
-                total = total + tab[rows, :]
-            total = total.T[0:FEATS]
-            high = total.astype(jnp.bfloat16)
-            low = (total - high.astype(jnp.float32)).astype(jnp.bfloat16)
-            parts.append(jnp.concatenate([high, low], axis=1))
-        wide_ref[...] = jnp.dot(jnp.concatenate(parts, axis=0), spread_ref[...], preferred_element_type=jnp.float32)
         lane = lax.broadcasted_iota(jnp.int32, (8, WIDTH), 1)
         which = lane % 9
         sub = lax.broadcasted_iota(jnp.int32, (8, WIDTH), 0)
-        for c in range(FINAL):
-            at = c * FEATS
-            eight = wide_ref[at : at + 8, :]
-            for j in range(1, 9):
-                eight = jnp.where(which == j, wide_ref[at + 8 * j : at + 8 * j + 8, :], eight)
-            last = jnp.sum(jnp.where(which == sub, wide_ref[at + 72 : at + 80, :], 0.0), axis=0, keepdims=True)
-            last = jnp.where(which[0:1] == 8, wide_ref[at + 80 : at + 81, :], last)
-            out_ref[0, 9 * c : 9 * c + 8, :] = eight
-            out_ref[0, 9 * c + 8 : 9 * c + 9, :] = last
+
+        def turned(part):
+            pieces = []
+            for c in range(part * PART, (part + 1) * PART):
+                rows = pl.ds(base + c * CAMS, CAMS)
+                total = start_ref[rows, :]
+                for tab in tabs:
+                    total = total + tab[rows, :]
+                total = total.T[0:FEATS]
+                high = total.astype(jnp.bfloat16)
+                low = (total - high.astype(jnp.float32)).astype(jnp.bfloat16)
+                pieces.append(jnp.concatenate([high, low], axis=1))
+            return jnp.concatenate(pieces, axis=0)
+
+        def spread_out(part, left):
+            rows = slice(part * PART * FEATS, (part + 1) * PART * FEATS)
+            wide_ref[rows, :] = jnp.dot(left, spread_ref[...], preferred_element_type=jnp.float32)
+
+        def pick(part):
+            for c in range(part * PART, (part + 1) * PART):
+                at = c * FEATS
+                eight = wide_ref[at : at + 8, :]
+                for j in range(1, 9):
+                    eight = jnp.where(which == j, wide_ref[at + 8 * j : at + 8 * j + 8, :], eight)
+                last = jnp.sum(jnp.where(which == sub, wide_ref[at + 72 : at + 80, :], 0.0), axis=0, keepdims=True)
+                last = jnp.where(which[0:1] == 8, wide_ref[at + 80 : at + 81, :], last)
+                out_ref[0, 9 * c : 9 * c + 8, :] = eight
+                out_ref[0, 9 * c + 8 : 9 * c + 9, :] = last
+
+        left = turned(0)
+        for part in range(FINAL // PART):
+            spread_out(part, left)
+            if part + 1 < FINAL // PART:
+                left = turned(part + 1)
+            if part:
+                pick(part - 1)
+        pick(FINAL // PART - 1)
 
 
 def params(**more):

time: 126 us -> 125 us (level)
  waiting for transfers between devices: 32.1 us -> 29.5 us
  Pallas kernels: 69.5 us -> 71.5 us
    pallas_call x1, Pallas kernels: 22.4 us -> 25.1 us  [schur(): pl.pallas_call(functools.partial(first_kernel, steps), grid=(steps + cell...]
    all_to_all x1, waiting for transfers between devices: 13.5 us -> 10.8 us  [local(): lax.all_to_all(pack(1, shares.reshape(SIDES, 2, PTS)), RC, 0, 0, tiled=True)]
  transfers between devices with their start and end apart: 3 -> 3, of which waited for: 3 -> 3; matrix products, arithmetic and copies ran while one was open for 3% -> 3% of each run, Pallas kernels for 28% -> 30%
where the time goes in v6:
time: 125 us; the launch traced here: 124 us
  Pallas kernels  71.5 us (57%)
  waiting for transfers between devices  29.5 us (24%)
  starting transfers between devices  18.6 us (15%)
  local copies, waits for them, and re-layouts  2.52 us (2%)
    pallas_call x1, Pallas kernels, schur(): pl.pallas_call(functools.partial(last_kernel, steps), grid=(steps + CAMS...  29.1 us
    pallas_call x1, Pallas kernels, schur(): pl.pallas_call(functools.partial(first_kernel, steps), grid=(steps + cell...  25.1 us
    all_to_all x1, waiting for transfers between devices, local(): in0 = lax.all_to_all(pack(0), RC, 0, 0, tiled=True)  17.7 us
    all_to_all x1, starting transfers between devices, local(): in0 = lax.all_to_all(pack(0), RC, 0, 0, tiled=True)  11.9 us
    all_to_all x1, waiting for transfers between devices, local(): lax.all_to_all(pack(1, shares.reshape(SIDES, 2, PTS)), RC, 0, 0, tiled=True)  10.8 us
    pallas_call x2, Pallas kernels, pack(): pl.pallas_call(functools.partial(pack_kernel, which), in_specs=[smem] * 3...  10.1 us
    pallas_call x1, Pallas kernels, local(): pl.pallas_call(rhs_kernel, in_specs=[smem] * 3 + [vmem] * 5, out_specs=vm...  7.11 us
    all_to_all x1, starting transfers between devices, local(): lax.all_to_all(pack(1, shares.reshape(SIDES, 2, PTS)), RC, 0, 0, tiled=True)  5.52 us
  transfers between devices with their start and end apart: 3, of which 3 were waited for; matrix products, arithmetic and copies ran while one was open for 3% of the time, Pallas kernels for 30%

profile of v6, /device:TPU:1, one launch (start us, length us, event | category | flops | bytes accessed | tf_op | source)
XLA Modules:
  0.0 123.9 jit_solution(15060614508828050403)
XLA Ops:
  0.6 4.8 %pack0.1 = f32[128,40,128]{2,1,0:T(8,128)} custom-call(s32[64]{0:T(128)} %bitcast.24, s32[2,64]{1,0:T(2,128)} %bitcast.21, s32[32]{0:T(128)} %refs_2_.3, f32[36,64,128]{2,1,0:T(8,128)} %bitcast.12, f32[12,64,128]{2,1,0:T(8,128)} %bitcast.16, f32[64,128]{1,0:T(8,128)} %refs_5_.3, s32[64,2,128]{2,1,0:T(2,128)} %refs_6_.3), custom_call_target="tpu_custom_call" | custom-call | flops 10000000 | bytes 6000000 | tf_op jit(solution)/shard_map/pack0/pallas_call | solution.py:433
  5.4 11.9 %all-to-all-start.1 = ((f32[128,40,128]{2,1,0:T(8,128)}), f32[128,40,128]{2,1,0:T(8,128)}, u32[]{:S(2)}, u32[]{:S(2)}) async-start(f32[128,40,128]{2,1,0:T(8,128)} %pack0.1), calls=%async_computation.1 | async-start | bytes 5242880 | tf_op jit(solution)/shard_map/all_to_all | solution.py:448
  17.3 7.1 %rhs.1 = f32[32,16,128]{2,1,0:T(8,128)} custom-call(s32[64]{0:T(128)} %bitcast.25, s32[2,64]{1,0:T(2,128)} %bitcast.22, s32[32]{0:T(128)} %refs_2_.3, f32[36,64,128]{2,1,0:T(8,128)} %bitcast.13, f32[12,64,128]{2,1,0:T(8,128)} %bitcast.17, f32[64,4,128]{2,1,0:T(4,128)} %res_ref.1, f32[64,128]{1,0:T(8,128)} %refs_5_.3, s32[64,2,128]{2,1,0:T(2,128)} %refs_6_.3), custom_call_target="tpu_custom_call" | custom-call | flops 10000000000 | bytes 3000000 | tf_op jit(solution)/shard_map/rhs/pallas_call | solution.py:450
  24.4 0.9 dynamic-slice_bitcast_fusion
  25.4 1.2 collective-permute-start
  26.6 1.0 collective-permute-done
  27.6 0.9 bitcast_add_fusion
  28.5 0.3 reshape.18
  28.8 0.2 copy.10
  29.0 1.1 reshape.19.refs_7_
  30.1 5.3 %pack1.1 = f32[128,40,128]{2,1,0:T(8,128)} custom-call(s32[64]{0:T(128)} %bitcast.26, s32[2,64]{1,0:T(2,128)} %bitcast.23, s32[32]{0:T(128)} %refs_2_.3, f32[36,64,128]{2,1,0:T(8,128)} %bitcast.14, f32[12,64,128]{2,1,0:T(8,128)} %bitcast.18, f32[64,128]{1,0:T(8,128)} %refs_5_.3, s32[64,2,128]{2,1,0:T(2,128)} %refs_6_.3, f32[128,2,128]{2,1,0:T(2,128)} %reshape.19.refs_7_), custom_call_target="tpu_custom_call" | custom-call | flops 10000000 | bytes 6000000 | tf_op jit(solution)/shard_map/pack1/pallas_call | solution.py:433
  35.4 17.7 %all-to-all-done.1.in_hbm.in_ref = f32[128,40,128]{2,1,0:T(8,128)} async-done(((f32[128,40,128]{2,1,0:T(8,128)}), f32[128,40,128]{2,1,0:T(8,128)}, u32[]{:S(2)}, u32[]{:S(2)}) %all-to-all-start.1) | async-done | bytes 2621472 | tf_op jit(solution)/shard_map/all_to_all | solution.py:448
  53.1 5.5 %all-to-all-start = ((f32[128,40,128]{2,1,0:T(8,128)}), f32[128,40,128]{2,1,0:T(8,128)}, u32[]{:S(2)}, u32[]{:S(2)}) async-start(f32[128,40,128]{2,1,0:T(8,128)} %pack1.1), calls=%async_computation | async-start | bytes 5242880 | tf_op jit(solution)/shard_map/all_to_all | solution.py:466
  58.6 25.1 %first.1.start_hbm = f32[16384,128]{1,0:T(8,128)} custom-call(f32[128,40,128]{2,1,0:T(8,128)} %all-to-all-done.1.in_hbm.in_ref, f32[128,40,128]{2,1,0:T(8,128)} %all-to-all-done.1.in_hbm.in_ref), custom_call_target="tpu_custom_call" | custom-call | flops 6000000000 | bytes 12000000 | tf_op jit(solution)/shard_map/first/pallas_call | solution.py:387
  83.8 10.8 %all-to-all-done.in_hbm.in_ref = f32[128,40,128]{2,1,0:T(8,128)} async-done(((f32[128,40,128]{2,1,0:T(8,128)}), f32[128,40,128]{2,1,0:T(8,128)}, u32[]{:S(2)}, u32[]{:S(2)}) %all-to-all-start) | async-done | bytes 2621472 | tf_op jit(solution)/shard_map/all_to_all | solution.py:466
  94.6 29.1 %last.1 = (f32[1,1152,1152]{2,1,0:T(8,128)}, f32[2,144]{1,0:T(2,128)}) custom-call(f32[128,40,128]{2,1,0:T(8,128)} %all-to-all-done.in_hbm.in_ref, f32[128,40,128]{2,1,0:T(8,128)} %all-to-all-done.in_hbm.in_ref, f32[16384,128]{1,0:T(8,128)} %first.1.start_hbm), custom_call_target="tpu_custom_call" | custom-call | flops 6000000000 | bytes 12000000 | tf_op jit(solution)/shard_map/last/pallas_call | solution.py:398
Async XLA Ops:
  5.4 47.7 %all-to-all-start.1 = ((f32[128,40,128]{2,1,0:T(8,128)}), f32[128,40,128]{2,1,0:T(8,128)}, u32[]{:S(2)}, u32[]{:S(2)}) async-start(f32[128,40,128]{2,1,0:T(8,128)} %pack0.1), calls=%async_computation.1 | async-start | bytes 5242880 | tf_op jit(solution)/shard_map/all_to_all | solution.py:448
  25.4 2.2 %collective-permute-start = (f32[16,16,128]{2,1,0:T(8,128)S(1)}, f32[16,16,128]{2,1,0:T(8,128)S(1)}, u32[]{:S(2)}, u32[]{:S(2)}) collective-permute-start(f32[16,16,128]{2,1,0:T(8,128)S(1)} %dynamic-slice_bitcast_fusion), channel_id=1, source_target_pairs={{0,1},{1,0},{2,3},{3,2},{4,5},{5,4},{6,7},{7,6},{8,9},{9,8},{10,11... | collective-permute-start | bytes 393224 | tf_op jit(solution)/shard_map/ppermute | solution.py:464
  53.1 41.5 %all-to-all-start = ((f32[128,40,128]{2,1,0:T(8,128)}), f32[128,40,128]{2,1,0:T(8,128)}, u32[]{:S(2)}, u32[]{:S(2)}) async-start(f32[128,40,128]{2,1,0:T(8,128)} %pack1.1), calls=%async_computation | async-start | bytes 5242880 | tf_op jit(solution)/shard_map/all_to_all | solution.py:466
